TPU v7x, 128 devices: a whole 4x4x4 slice. The times are simulated.
128 devices in a mesh: seq: 32 (over z, y, core), grp: 4 (over x).
Axes of the slice: x: 4, y: 4, z: 4, core: 2. Of those that a mesh axis runs over, the one named last changes fastest.
Arguments:
- query_states: bfloat16 [64, 16384, 128], P('grp', 'seq'), may hold values from -6 to 6
- key_states: bfloat16 [8, 16384, 128], P('grp', 'seq'), may hold values from -6 to 6
- value_states: bfloat16 [8, 16384, 128], P('grp', 'seq'), may hold values from -6 to 6
- tile_keys: int32 [64, 128, 16], P('grp'), may hold values from 0 to 127, as said below
- tile_count: int32 [64, 128], P('grp'), may hold values from 1 to 16, as said below
- out_weight: bfloat16 [8192, 4096], P('grp'), may hold values from -0.0625 to 0.0625
Outputs:
- projected: bfloat16 [16384, 4096], P(('seq', 'grp'))
Inputs may be any that keep to these rules, and one draw needn't show every extreme that they name: `tile_count`: for each head and query block, at least one and at most 16 key blocks are named; 16 is reached. `tile_keys`: for head h and query block i, slots 0 to tile_count[h, i] - 1 name distinct key blocks in falling order, the first being block i itself and none after i; the remaining slots hold 0.
All inputs are finite; a program needn't handle non-finite values.
Results may differ from a plain program's by a relative error of at most 0.0056.
Values may be sent and summed in bfloat16 or wider, within the bound.
No kernel may reach another device: no remote copies, remote signals or barrier semaphores. Data moves between devices by JAX's collectives and lax.ppermute only.
A program may use at most 128 MiB of HBM per device.

v0:
```python
import functools
import math

import jax
import jax.numpy as jnp
from jax import lax
from jax.experimental import pallas as pl
from jax.experimental.pallas import tpu as pltpu
from jax.sharding import PartitionSpec as P

BLK = 128
SLOTS = 16
PAIR = 2 * BLK
SPAN = SLOTS * BLK
RING = 4
CORES = 2
SEQ_DEVICES = RING * RING * CORES
SIDE_COUPLES = 4
CHUNK_COUPLES = 2 * SIDE_COUPLES
EXP2_SCALE = float(BLK ** -0.5 * math.log2(math.e))
LOW = -1e30
MIB = 2**20

SHORT = pl.CostEstimate(flops=1, bytes_accessed=1, transcendentals=0)
MIDDLE = pl.CostEstimate(flops=2 * 10**9, bytes_accessed=10**7, transcendentals=0)

VMEM = pl.BlockSpec(memory_space=pltpu.VMEM)
HBM = pl.BlockSpec(memory_space=pltpu.HBM)


def stay(array):
    return pltpu.with_memory_space_constraint(array, pltpu.HBM)


def cat(parts, axis):
    return jnp.concatenate(parts, axis)


def score_couple(couple, lists, counts, place, q_ref, table, score_ref, top_ref):
    key_row = lax.broadcasted_iota(jnp.int32, (BLK, PAIR), 0)
    query_row = lax.broadcasted_iota(jnp.int32, (BLK, PAIR), 1) % BLK
    zero = jnp.zeros((BLK, BLK), jnp.bfloat16)
    chunk = couple // CHUNK_COUPLES
    side = couple // SIDE_COUPLES % 2
    head = 2 * (couple % SIDE_COUPLES)
    rows = pl.ds(pl.multiple_of(place[1 + side * RING + chunk] * BLK, BLK), BLK)
    qa = q_ref[side, head, rows, :].T
    qb = q_ref[side, head + 1, rows, :].T
    queries = cat([cat([qa, zero], 1), cat([zero, qb], 1)], 0)
    a = 2 * couple * SLOTS
    keys = cat(
        [cat([table[lists[a + n]], table[lists[a + SLOTS + n]]], 1) for n in range(SLOTS)], 0
    )
    scores = jnp.dot(keys, queries, preferred_element_type=jnp.float32)
    count = live_counts(couple, counts)
    top = None
    for n in range(SLOTS):
        tile = scores[n * BLK : (n + 1) * BLK]
        if n == 0:
            tile = jnp.where(key_row <= query_row, tile, LOW)
            top = tile.reshape(16, 8, PAIR).max(0)
        else:
            best = tile.reshape(16, 8, PAIR).max(0)
            top = jnp.maximum(top, jnp.where(n < count, best, LOW))
        score_ref[n * BLK : (n + 1) * BLK, :] = tile
    top_ref[...] = jnp.max(top, axis=0, keepdims=True)


def live_counts(couple, counts):
    lane = lax.broadcasted_iota(jnp.int32, (1, PAIR), 1)
    return jnp.where(lane < BLK, counts[2 * couple], counts[2 * couple + 1])


def weigh_couple(couple, counts, score_ref, top_ref):
    count = live_counts(couple, counts)
    top = top_ref[...]
    total = jnp.zeros((8, PAIR), jnp.float32)
    tiles = []
    for n in range(SLOTS):
        shift = top if n == 0 else jnp.where(n < count, top, -LOW)
        weights = jnp.exp2((score_ref[n * BLK : (n + 1) * BLK, :] - shift) * EXP2_SCALE)
        total += weights.reshape(16, 8, PAIR).sum(0)
        tiles.append(weights.astype(jnp.bfloat16))
    return tiles, jnp.sum(total, axis=0, keepdims=True)


def combine_couple(couple, weights, total, lists, values, out_ref):
    head = 2 * (couple % SIDE_COUPLES)
    for half in range(2):
        pair = 2 * couple + half
        tiles = cat([values[lists[pair * SLOTS + n]] for n in range(SLOTS)], 1)
        lanes = slice(half * BLK, (half + 1) * BLK)
        summed = jnp.dot(tiles, weights[:, lanes], preferred_element_type=jnp.float32)
        attended = (summed / total[:, lanes]).T.astype(jnp.bfloat16)
        cols = pl.ds(pl.multiple_of((head + half) * BLK, BLK), BLK)
        out_ref[:, cols] = attended


def pipelined(first, score, weigh, buffers, rest):
    score_a, top_a, score_b, top_b = buffers
    score(first, score_a, top_a)
    for copy in rest:
        copy.wait()

    last = first + SIDE_COUPLES - 1

    def step(index, carry):
        couple = first + 2 * index
        score(couple + 1, score_b, top_b)
        weigh(couple, score_a, top_a)
        score(jnp.minimum(couple + 2, last), score_a, top_a)
        weigh(couple + 1, score_b, top_b)
        return carry

    lax.fori_loop(0, SIDE_COUPLES // 2, step, 0)


BUFFERS = [pltpu.VMEM((SPAN, PAIR), jnp.float32), pltpu.VMEM((1, PAIR), jnp.float32)] * 2


def hold_kernel(source_ref, after_ref, out_ref, sem):
    copy = pltpu.make_async_copy(source_ref, out_ref, sem)
    copy.start()
    copy.wait()


def hold_call(source, after):
    return pl.pallas_call(
        hold_kernel,
        name="hold_weight",
        in_specs=[HBM, HBM],
        out_specs=VMEM,
        out_shape=pltpu.VMEM(source.shape, source.dtype),
        scratch_shapes=[pltpu.SemaphoreType.DMA],
        compiler_params=pltpu.CompilerParams(vmem_limit_bytes=4 * MIB),
    )(stay(source), after)


def prepare_kernel(key_ref, value_ref, mine_ref, theirs_ref, key_held, value_held, sems):
    core = lax.rem(lax.axis_index("seq"), CORES)
    copies = [
        pltpu.make_async_copy(key_ref, key_held, sems.at[0]),
        pltpu.make_async_copy(value_ref, value_held, sems.at[1]),
    ]
    for copy in copies:
        copy.start()
    for copy in copies:
        copy.wait()
    for out_ref, head in ((mine_ref, core), (theirs_ref, 1 - core)):
        for block in range(out_ref.shape[1]):
            rows = slice(block * BLK, (block + 1) * BLK)
            out_ref[0, block] = key_held[head, rows, :]
            out_ref[1, block] = value_held[head, rows, :].T


def prepare_call(keys, values):
    blocks = keys.shape[1] // BLK
    shape = jax.ShapeDtypeStruct((2, blocks, BLK, BLK), jnp.bfloat16)
    return pl.pallas_call(
        prepare_kernel,
        name="prepare",
        in_specs=[HBM] * 2,
        out_specs=[VMEM] * 2,
        out_shape=[shape, shape],
        scratch_shapes=[pltpu.VMEM(keys.shape, keys.dtype)] * 2
        + [pltpu.SemaphoreType.DMA((2,))],
        compiler_params=pltpu.CompilerParams(vmem_limit_bytes=6 * MIB),
        cost_estimate=SHORT,
    )(stay(keys), stay(values))


def bring(pieces, tables, sems, places):
    copies = []
    for index, (piece, (table, at)) in enumerate(zip(pieces, places)):
        copies.append(
            pltpu.make_async_copy(
                piece, tables[table].at[pl.ds(at, piece.shape[0])], sems.at[index]
            )
        )
    for copy in copies:
        copy.start()
    return copies


def tables_kernel(places, *refs):
    pieces, tables, sems = refs[: len(places)], refs[len(places) : -1], refs[-1]
    for copy in bring(pieces, tables, sems, places):
        copy.wait()


def tables_call(places, pieces):
    return pl.pallas_call(
        functools.partial(tables_kernel, places),
        name="tables",
        in_specs=[HBM] * len(pieces),
        out_specs=[VMEM] * 2,
        out_shape=[pltpu.VMEM((BLK, BLK, BLK), jnp.bfloat16)] * 2,
        scratch_shapes=[pltpu.SemaphoreType.DMA((len(pieces),))],
        compiler_params=pltpu.CompilerParams(vmem_limit_bytes=4 * MIB),
        cost_estimate=SHORT,
    )(*map(stay, pieces))


def attend_kernel(first, places, lists, counts, place, q_ref, after_ref, also_ref, *refs):
    if places:
        pieces, refs = refs[: len(places)], refs[len(places) + 2 :]
        out_ref, keys, values, *buffers, sems = refs
        copies = bring(pieces, (keys, values), sems, places)
        copies[0].wait()
        rest = copies[1:]
    else:
        keys, values, out_ref, *buffers = refs
        rest = []

    def score(couple, score_ref, top_ref):
        score_couple(couple, lists, counts, place, q_ref, keys, score_ref, top_ref)

    def weigh(couple, score_ref, top_ref):
        tiles, total = weigh_couple(couple, counts, score_ref, top_ref)
        combine_couple(couple, cat(tiles, 0), total, lists, values, out_ref)

    pipelined(first, score, weigh, buffers, rest)


def attend_call(
    name, chunk, side, lists, counts, place, queries, after, tables, pieces=(), places=(), cost=SHORT
):
    out_shape = [jax.ShapeDtypeStruct((BLK, 8 * BLK), jnp.bfloat16)]
    scratch = list(BUFFERS)
    aliases = {}
    if pieces:
        out_shape += [pltpu.VMEM(table.shape, table.dtype) for table in tables]
        scratch += [pltpu.SemaphoreType.DMA((len(pieces),))]
        aliases = {6 + len(pieces): 1, 7 + len(pieces): 2}
    return pl.pallas_call(
        functools.partial(attend_kernel, chunk * CHUNK_COUPLES + side * SIDE_COUPLES, places),
        name=name,
        grid_spec=pltpu.PrefetchScalarGridSpec(
            num_scalar_prefetch=3,
            grid=(1,),
            in_specs=[VMEM] + [VMEM if pieces else HBM] * 2 + [HBM] * len(pieces) + [VMEM] * len(tables),
            out_specs=[VMEM] * len(out_shape),
            scratch_shapes=scratch,
        ),
        out_shape=out_shape,
        input_output_aliases=aliases,
        compiler_params=pltpu.CompilerParams(vmem_limit_bytes=10 * MIB),
        cost_estimate=cost,
    )(lists, counts, place, queries, *after, *map(stay, pieces), *tables)


def queries_kernel(place, source_ref, after_ref, mine_ref, theirs_ref, sems):
    heads = mine_ref.shape[0]
    core = place[0]
    copies = [
        pltpu.make_async_copy(
            source_ref.at[pl.ds(owner * heads, heads)], out_ref, sems.at[index]
        )
        for index, (owner, out_ref) in enumerate(((core, mine_ref), (1 - core, theirs_ref)))
    ]
    for copy in copies:
        copy.start()
    for copy in copies:
        copy.wait()


def queries_call(place, queries, heads, after):
    shape = jax.ShapeDtypeStruct((heads,) + queries.shape[1:], queries.dtype)
    return pl.pallas_call(
        queries_kernel,
        name="queries",
        grid_spec=pltpu.PrefetchScalarGridSpec(
            num_scalar_prefetch=1,
            grid=(1,),
            in_specs=[HBM, HBM],
            out_specs=[VMEM, VMEM],
            scratch_shapes=[pltpu.SemaphoreType.DMA((2,))],
        ),
        out_shape=[shape, shape],
        compiler_params=pltpu.CompilerParams(vmem_limit_bytes=8 * MIB),
        cost_estimate=SHORT,
    )(place, stay(queries), after)


def project_kernel(kind, place, mine_ref, theirs_ref, held_ref, after_ref, *refs):
    out_ref = refs[-1]
    width = held_ref.shape[1]
    tile = 1024
    core = place[0]
    mine = mine_ref[...]
    theirs = theirs_ref[...]
    both = cat([jnp.where(core == 0, mine, theirs), jnp.where(core == 0, theirs, mine)], 1)
    for at in range(0, width, tile):
        cols = slice(at, at + tile)
        total = jnp.dot(both, held_ref[:, cols], preferred_element_type=jnp.float32)
        if kind in ("first", "own"):
            total = total + refs[0][:, cols].astype(jnp.float32)
        out_ref[:, cols] = total.astype(out_ref.dtype)


def project_call(kind, place, mine, theirs, held, after, *arrived):
    width = held.shape[1]
    out_type = jnp.float32 if kind == "own" else jnp.bfloat16
    return pl.pallas_call(
        functools.partial(project_kernel, kind),
        name="project_" + kind,
        grid_spec=pltpu.PrefetchScalarGridSpec(
            num_scalar_prefetch=1,
            grid=(1,),
            in_specs=[VMEM] * 3 + [HBM] + [VMEM] * len(arrived),
            out_specs=VMEM,
        ),
        out_shape=jax.ShapeDtypeStruct((BLK, width), out_type),
        compiler_params=pltpu.CompilerParams(vmem_limit_bytes=8 * MIB),
        cost_estimate=MIDDLE if kind == "own" else SHORT,
    )(place, mine, theirs, held, after, *arrived)


def chip_perm(phase, step):
    pairs = []
    for z in range(RING):
        for y in range(RING):
            for core in range(CORES):
                if (core == 0) == (phase == 0):
                    to_z, to_y = z, (y + step) % RING
                else:
                    to_z, to_y = (z + step) % RING, y
                pairs.append(((z * RING + y) * CORES + core, (to_z * RING + to_y) * CORES + core))
    return pairs


SWAP = [(i, i ^ 1) for i in range(SEQ_DEVICES)]


def along(array, phase, step):
    return lax.ppermute(array, "seq", chip_perm(phase, step))


def swap(array):
    return lax.ppermute(array, "seq", SWAP)


def turn(array, step):
    pairs = []
    for seq in range(SEQ_DEVICES):
        way = step if seq % CORES == 0 else -step
        pairs += [(seq * RING + i, seq * RING + (i + way) % RING) for i in range(RING)]
    return lax.ppermute(array, ("seq", "grp"), pairs)


def gather_tiles(own):
    parts = [own, along(own, 0, 1), along(own, 0, -1), along(own, 0, 2)]
    keys = cat([part[0] for part in parts], 0)
    values = cat([part[1] for part in parts], 0)
    keys_left, values_right = along(keys, 1, 1), along(values, 1, -1)
    values_left, keys_right = along(values, 1, 1), along(keys, 1, -1)
    keys_far, values_far = along(keys_left, 1, 1), along(values_right, 1, -1)
    size = keys.shape[0]
    early = [keys, keys_left, keys_right, values, values_left, values_right]
    early_places = ((0, 0), (0, size), (0, 2 * size), (1, 0), (1, size), (1, 2 * size))
    late = [keys_far, values_far]
    late_places = ((0, 3 * size), (1, 3 * size))
    return parts[1], early, early_places, late, late_places


def body(query_states, key_states, value_states, tile_keys, tile_count, out_weight):
    head_group, row_count, width = query_states.shape
    kv_group = key_states.shape[0]
    blocks = row_count // BLK
    heads = head_group // kv_group
    seq_place = lax.axis_index("seq")
    grp_place = lax.axis_index("grp")
    core = seq_place % CORES
    chip = seq_place // CORES
    chip_z, chip_y = chip // RING, chip % RING

    ways = jnp.array([[2, 1, 3, 0], [2, 3, 1, 0]], jnp.int32)
    mine_chunks = jnp.where(core == 0, ways[0], ways[1])
    theirs_chunks = jnp.where(core == 0, ways[1], ways[0])
    chunks = (grp_place + jnp.stack([theirs_chunks, mine_chunks])) % RING
    place = jnp.concatenate([core[None], chunks.reshape(-1)]).astype(jnp.int32)
    mine, theirs = prepare_call(key_states, value_states)
    neighbor, early, early_places, late, late_places = gather_tiles(cat([mine, swap(theirs)], 1))

    queries_mine, queries_theirs = queries_call(place, query_states, heads, neighbor)
    queries = jnp.stack([swap(queries_theirs), queries_mine])

    sides = jnp.stack([1 - core, core])
    order = (chip * 2 * blocks + sides[None, :] * blocks + chunks.T).reshape(-1)
    my_lists = lax.dynamic_slice_in_dim(tile_keys, core * heads, heads, 0)
    my_counts = lax.dynamic_slice_in_dim(tile_count, core * heads, heads, 0)
    lists = jnp.swapaxes(jnp.take(my_lists, order, axis=1), 0, 1)
    counts = jnp.swapaxes(jnp.take(my_counts, order, axis=1), 0, 1).reshape(-1)

    span = 2 * blocks
    from_chip = lists // span
    inside = lists % span
    step_z = (from_chip // RING - chip_z) % RING
    step_y = (from_chip % RING - chip_y) % RING

    def arrival(step):
        return jnp.where(step == 1, 2, jnp.where(step == 2, 3, jnp.where(step == 3, 1, 0)))

    inner = arrival(jnp.where(core == 0, step_y, step_z))
    outer = arrival(jnp.where(core == 0, step_z, step_y))
    lists = (
        (outer * RING + inner) * span
        + (inside // blocks + core) % CORES * blocks
        + inside % blocks
    ).reshape(-1)

    held = hold_call(out_weight, neighbor)

    tables = tables_call(early_places, early)
    far_theirs, *tables = attend_call(
        "far_theirs", 0, 0, lists, counts, place, queries, (held, held), tables, late, late_places
    )

    def attend(name, chunk, side, after, cost=SHORT):
        (out,) = attend_call(
            name, chunk, side, lists, counts, place, queries, after, tables, cost=cost
        )
        return out

    far_mine = attend("far_mine", 0, 1, (far_theirs, far_theirs))
    far = project_call("far", place, far_mine, swap(far_theirs), held, far_mine)
    passed = turn(far, 1)
    first_theirs = attend("first_theirs", 1, 0, (far, far))
    first_mine = attend("first_mine", 1, 1, (first_theirs, first_theirs))
    second_theirs = attend("second_theirs", 2, 0, (first_mine, first_mine))
    first = project_call(
        "first", place, first_mine, swap(first_theirs), held, second_theirs, passed
    )
    arrived = turn(first, 1)
    second_mine = attend("second_mine", 2, 1, (first, first))
    second = project_call(
        "second", place, second_mine, swap(second_theirs), held, second_mine
    )
    arrived_last = turn(second, -1)
    own_theirs = attend("own_theirs", 3, 0, (second, second))
    own_mine = attend("own_mine", 3, 1, (own_theirs, own_theirs))
    own = project_call("own", place, own_mine, swap(own_theirs), held, own_mine, arrived)
    total = own + arrived_last.astype(jnp.float32)
    return total.astype(jnp.bfloat16)


def solution(mesh):
    placed = (
        P("grp", "seq", None),
        P("grp", "seq", None),
        P("grp", "seq", None),
        P("grp", None, None),
        P("grp", None),
        P("grp", None),
    )
    return jax.shard_map(
        body, mesh=mesh, in_specs=placed, out_specs=P(("seq", "grp"), None), check_vma=False
    )
```

profile of v0, /device:TPU:1, one launch (start us, length us, event | category | flops | bytes accessed | tf_op | source)
XLA Modules:
  0.0 124.7 jit_solution(8210020662307036194)
XLA Ops:
  0.0 1.2 prepare.1
  1.2 1.5 %collective-permute-start = (bf16[2,4,128,128]{3,2,1,0:T(8,128)(2,1)S(1)}, bf16[2,4,128,128]{3,2,1,0:T(8,128)(2,1)S(1)}, u32[]{:S(2)}, u32[]{:S(2)}) collective-permute-start(bf16[2,4,128,128]{3,2,1,0:T(8,128)(2,1)S(1)} %get-tuple-element.15), channel_id=1, source_target_pairs={{0,4},{4,0},{8,12},{12,8},{16,20},{20,16},{24,28},{28,24},{32,36},... | collective-permute-start | bytes 786440 | tf_op jit(solution)/shard_map/ppermute | solution.py:340
  3.9 3.8 %collective-permute-start.4 = (bf16[2,8,128,128]{3,2,1,0:T(8,128)(2,1)S(1)}, bf16[2,8,128,128]{3,2,1,0:T(8,128)(2,1)S(1)}, u32[]{:S(2)}, u32[]{:S(2)}) collective-permute-start(bf16[2,8,128,128]{3,2,1,0:T(8,128)(2,1)S(1)} %constant_dynamic-update-slice_fusion), channel_id=1, source_target_pairs={{0,16},{4,68},{8,24},{12,76},{16,0},{20,84},{24,8},{28,92},{32,48}... | collective-permute-start | bytes 1572872 | tf_op jit(solution)/shard_map/ppermute | solution.py:336
  9.2 5.4 %collective-permute-done.4 = bf16[2,8,128,128]{3,2,1,0:T(8,128)(2,1)S(1)} collective-permute-done((bf16[2,8,128,128]{3,2,1,0:T(8,128)(2,1)S(1)}, bf16[2,8,128,128]{3,2,1,0:T(8,128)(2,1)S(1)}, u32[]{:S(2)}, u32[]{:S(2)}) %collective-permute-start.4) | collective-permute-done | bytes 524320 | tf_op jit(solution)/shard_map/ppermute | solution.py:336
  14.6 6.1 %collective-permute-done.3 = bf16[2,8,128,128]{3,2,1,0:T(8,128)(2,1)S(1)} collective-permute-done((bf16[2,8,128,128]{3,2,1,0:T(8,128)(2,1)S(1)}, bf16[2,8,128,128]{3,2,1,0:T(8,128)(2,1)S(1)}, u32[]{:S(2)}, u32[]{:S(2)}) %collective-permute-start.3) | collective-permute-done | bytes 524320 | tf_op jit(solution)/shard_map/ppermute | solution.py:336
  24.3 1.5 %collective-permute-start.7 = (bf16[32,128,128]{2,1,0:T(8,128)(2,1)}, bf16[32,128,128]{2,1,0:T(8,128)(2,1)}, u32[]{:S(2)}, u32[]{:S(2)}) collective-permute-start(bf16[32,128,128]{2,1,0:T(8,128)(2,1)} %pad_maximum_fusion.2.refs_3_), channel_id=1, source_target_pairs={{0,96},{4,28},{8,104},{12,4},{16,112},{20,12},{24,120},{28,20},{32... | collective-permute-start | bytes 3145736 | tf_op jit(solution)/shard_map/ppermute | solution.py:336
  26.6 1.4 %collective-permute-start.9 = (bf16[32,128,128]{2,1,0:T(8,128)(2,1)}, bf16[32,128,128]{2,1,0:T(8,128)(2,1)}, u32[]{:S(2)}, u32[]{:S(2)}) collective-permute-start(bf16[32,128,128]{2,1,0:T(8,128)(2,1)} %pad_maximum_fusion.1.refs_0_), channel_id=1, source_target_pairs={{0,96},{4,28},{8,104},{12,4},{16,112},{20,12},{24,120},{28,20},{32... | collective-permute-start | bytes 3145736 | tf_op jit(solution)/shard_map/ppermute | solution.py:336
  28.0 2.1 %queries.1 = (bf16[8,512,128]{2,1,0:T(8,128)(2,1)S(1)}, bf16[8,512,128]{2,1,0:T(8,128)(2,1)S(1)}) custom-call(s32[9]{0:T(128)S(1)} %pad_add_fusion.place, bf16[16,512,128]{2,1,0:T(8,128)(2,1)} %source_ref.2, bf16[2,8,128,128]{3,2,1,0:T(8,128)(2,1)S(1)} %collective-permute-done.1.after_ref), custom_call_target="tpu_custom_call" | custom-call | flops 1 | bytes 1 | tf_op jit(solution)/shard_map/queries/pallas_call | solution.py:269
  30.1 2.4 %collective-permute-start.2 = (bf16[8,512,128]{2,1,0:T(8,128)(2,1)S(1)}, bf16[8,512,128]{2,1,0:T(8,128)(2,1)}, u32[]{:S(2)}, u32[]{:S(2)}) collective-permute-start(bf16[8,512,128]{2,1,0:T(8,128)(2,1)S(1)} %get-tuple-element.16), channel_id=1, source_target_pairs={{0,4},{4,0},{8,12},{12,8},{16,20},{20,16},{24,28},{28,24},{32,36},... | collective-permute-start | bytes 3145736 | tf_op jit(solution)/shard_map/ppermute | solution.py:340
  32.5 4.9 %collective-permute-done.5.refs_1_ = bf16[32,128,128]{2,1,0:T(8,128)(2,1)} collective-permute-done((bf16[32,128,128]{2,1,0:T(8,128)(2,1)}, bf16[32,128,128]{2,1,0:T(8,128)(2,1)}, u32[]{:S(2)}, u32[]{:S(2)}) %collective-permute-start.5) | collective-permute-done | bytes 1048608 | tf_op jit(solution)/shard_map/ppermute | solution.py:336
  38.6 2.7 %collective-permute-start.8 = (bf16[32,128,128]{2,1,0:T(8,128)(2,1)}, bf16[32,128,128]{2,1,0:T(8,128)(2,1)}, u32[]{:S(2)}, u32[]{:S(2)}) collective-permute-start(bf16[32,128,128]{2,1,0:T(8,128)(2,1)} %collective-permute-done.7.refs_5_), channel_id=1, source_target_pairs={{0,96},{4,28},{8,104},{12,4},{16,112},{20,12},{24,120},{28,20},{32... | collective-permute-start | bytes 3145736 | tf_op jit(solution)/shard_map/ppermute | solution.py:336
  43.1 5.8 %hold_weight.1.after_ref.also_ref.held_ref = bf16[2048,4096]{1,0:T(8,128)(2,1)S(1)} custom-call(bf16[2048,4096]{1,0:T(8,128)(2,1)} %source_ref.3, bf16[2,8,128,128]{3,2,1,0:T(8,128)(2,1)S(1)} %collective-permute-done.1.after_ref), custom_call_target="tpu_custom_call" | custom-call | tf_op jit(solution)/shard_map/hold_weight/pallas_call | solution.py:128
  49.8 2.9 %tables.1 = (bf16[128,128,128]{2,1,0:T(8,128)(2,1)S(1)}, bf16[128,128,128]{2,1,0:T(8,128)(2,1)S(1)}) custom-call(bf16[32,128,128]{2,1,0:T(8,128)(2,1)} %pad_maximum_fusion.1.refs_0_, bf16[32,128,128]{2,1,0:T(8,128)(2,1)} %collective-permute-done.5.refs_1_, bf16[32,128,128]{2,1,0:T(8,128)(2,1)} %collective-permute-done.9.refs_2_, ...), custom_call_target="tpu_custom_call" | custom-call | flops 1 | bytes 1 | tf_op jit(solution)/shard_map/tables/pallas_call | solution.py:192
  52.7 1.4 %pad_maximum_fusion.q_ref = bf16[2,8,512,128]{3,2,1,0:T(8,128)(2,1)S(1)} fusion(bf16[1,8,512,128]{3,2,1,0:T(8,128)(2,1)S(1)} %bitcast.24, bf16[1,8,512,128]{3,2,1,0:T(8,128)(2,1)} %bitcast.4), kind=kLoop, calls=%fused_computation.2 | loop fusion | flops 1048576 | bytes 4194304 | tf_op jit(solution)/shard_map/stack | solution.py:386
  54.1 5.8 %collective-permute-done.6.refs_0_ = bf16[32,128,128]{2,1,0:T(8,128)(2,1)} collective-permute-done((bf16[32,128,128]{2,1,0:T(8,128)(2,1)}, bf16[32,128,128]{2,1,0:T(8,128)(2,1)}, u32[]{:S(2)}, u32[]{:S(2)}) %collective-permute-start.6) | collective-permute-done | bytes 1048608 | tf_op jit(solution)/shard_map/ppermute | solution.py:336
  61.0 5.8 %far_theirs.1 = (bf16[128,1024]{1,0:T(8,128)(2,1)S(1)}, bf16[128,128,128]{2,1,0:T(8,128)(2,1)S(1)}, bf16[128,128,128]{2,1,0:T(8,128)(2,1)S(1)}) custom-call(s32[1024]{0:T(1024)S(1)} %reshape.71.lists, s32[64]{0:T(128)S(1)} %reshape.72.counts, s32[9]{0:T(128)S(1)} %pad_add_fusion.place, ...), custom_call_target="tpu_custom_call", output_to_operand_aliasing={{1}: (8, {}), {2}: (9, {})} | custom-call | flops 1 | bytes 1 | tf_op jit(solution)/shard_map/far_theirs/pallas_call | solution.py:235
  66.8 2.1 %collective-permute-start.11 = (bf16[128,1024]{1,0:T(8,128)(2,1)S(1)}, bf16[128,1024]{1,0:T(8,128)(2,1)S(1)}, u32[]{:S(2)}, u32[]{:S(2)}) collective-permute-start(bf16[128,1024]{1,0:T(8,128)(2,1)S(1)} %get-tuple-element.20.after_ref.also_ref), channel_id=1, source_target_pairs={{0,4},{4,0},{8,12},{12,8},{16,20},{20,16},{24,28},{28,24},{32,36},... | collective-permute-start | bytes 786440 | tf_op jit(solution)/shard_map/ppermute | solution.py:340
  68.9 4.5 %far_mine.1.mine_ref.after_ref = bf16[128,1024]{1,0:T(8,128)(2,1)S(1)} custom-call(s32[1024]{0:T(1024)S(1)} %reshape.71.lists, s32[64]{0:T(128)S(1)} %reshape.72.counts, s32[9]{0:T(128)S(1)} %pad_add_fusion.place, bf16[2,8,512,128]{3,2,1,0:T(8,128)(2,1)S(1)} %pad_maximum_fusion.q_ref, bf16[128,1024]{1,0:T(8,128)(2,1)S(1)} %get-tuple-element.20.after_ref.also_ref, ...), custom_call_target="tpu_custom_call" | custom-call | flops 1 | bytes 1 | tf_op jit(solution)/shard_map/far_mine/pallas_call | solution.py:235
  73.5 3.0 %project_far.1.after_ref.also_ref = bf16[128,4096]{1,0:T(8,128)(2,1)S(1)} custom-call(s32[9]{0:T(128)S(1)} %pad_add_fusion.place, bf16[128,1024]{1,0:T(8,128)(2,1)S(1)} %far_mine.1.mine_ref.after_ref, bf16[128,1024]{1,0:T(8,128)(2,1)S(1)} %collective-permute-done.11.theirs_ref, bf16[2048,4096]{1,0:T(8,128)(2,1)S(1)} %hold_weight.1.after_ref.also_ref.held_ref, ...), custom_call_target="tpu_custom_call" | custom-call | flops 1 | bytes 1 | tf_op jit(solution)/shard_map/project_far/pallas_call | solution.py:304
  76.5 2.7 %collective-permute-start.13 = (bf16[128,4096]{1,0:T(8,128)(2,1)S(1)}, bf16[128,4096]{1,0:T(8,128)(2,1)S(1)}, u32[]{:S(2)}, u32[]{:S(2)}) collective-permute-start(bf16[128,4096]{1,0:T(8,128)(2,1)S(1)} %project_far.1.after_ref.also_ref), channel_id=1, source_target_pairs={{0,1},{1,2},{2,3},{3,0},{4,7},{5,4},{6,5},{7,6},{8,9},{9,10},{10,1... | collective-permute-start | bytes 3145736 | tf_op jit(solution)/shard_map/ppermute | solution.py:348
  79.2 4.5 %first_theirs.1.after_ref.also_ref = bf16[128,1024]{1,0:T(8,128)(2,1)S(1)} custom-call(s32[1024]{0:T(1024)S(1)} %reshape.71.lists, s32[64]{0:T(128)S(1)} %reshape.72.counts, s32[9]{0:T(128)S(1)} %pad_add_fusion.place, bf16[2,8,512,128]{3,2,1,0:T(8,128)(2,1)S(1)} %pad_maximum_fusion.q_ref, bf16[128,4096]{1,0:T(8,128)(2,1)S(1)} %project_far.1.after_ref.also_ref, ...), custom_call_target="tpu_custom_call" | custom-call | flops 1 | bytes 1 | tf_op jit(solution)/shard_map/first_theirs/pallas_call | solution.py:235
  83.9 4.5 %first_mine.1.after_ref.also_ref.mine_ref = bf16[128,1024]{1,0:T(8,128)(2,1)S(1)} custom-call(s32[1024]{0:T(1024)S(1)} %reshape.71.lists, s32[64]{0:T(128)S(1)} %reshape.72.counts, s32[9]{0:T(128)S(1)} %pad_add_fusion.place, bf16[2,8,512,128]{3,2,1,0:T(8,128)(2,1)S(1)} %pad_maximum_fusion.q_ref, bf16[128,1024]{1,0:T(8,128)(2,1)S(1)} %first_theirs.1.after_ref.also_ref, ...), custom_call_target="tpu_custom_call" | custom-call | flops 1 | bytes 1 | tf_op jit(solution)/shard_map/first_mine/pallas_call | solution.py:235
  88.4 4.5 %second_theirs.1.after_ref = bf16[128,1024]{1,0:T(8,128)(2,1)S(1)} custom-call(s32[1024]{0:T(1024)S(1)} %reshape.71.lists, s32[64]{0:T(128)S(1)} %reshape.72.counts, s32[9]{0:T(128)S(1)} %pad_add_fusion.place, bf16[2,8,512,128]{3,2,1,0:T(8,128)(2,1)S(1)} %pad_maximum_fusion.q_ref, bf16[128,1024]{1,0:T(8,128)(2,1)S(1)} %first_mine.1.after_ref.also_ref.mine_ref, ...), custom_call_target="tpu_custom_call" | custom-call | flops 1 | bytes 1 | tf_op jit(solution)/shard_map/second_theirs/pallas_call | solution.py:235
  93.5 3.0 %project_first.1.after_ref.also_ref = bf16[128,4096]{1,0:T(8,128)(2,1)S(1)} custom-call(s32[9]{0:T(128)S(1)} %pad_add_fusion.place, bf16[128,1024]{1,0:T(8,128)(2,1)S(1)} %first_mine.1.after_ref.also_ref.mine_ref, bf16[128,1024]{1,0:T(8,128)(2,1)S(1)} %collective-permute-done.12.theirs_ref, bf16[2048,4096]{1,0:T(8,128)(2,1)S(1)} %hold_weight.1.after_ref.also_ref.held_ref, ...), custom_call_target="tpu_custom_call" | custom-call | flops 1 | bytes 1 | tf_op jit(solution)/shard_map/project_first/pallas_call | solution.py:304
  97.4 4.5 %second_mine.1.mine_ref.after_ref = bf16[128,1024]{1,0:T(8,128)(2,1)S(1)} custom-call(s32[1024]{0:T(1024)S(1)} %reshape.71.lists, s32[64]{0:T(128)S(1)} %reshape.72.counts, s32[9]{0:T(128)S(1)} %pad_add_fusion.place, bf16[2,8,512,128]{3,2,1,0:T(8,128)(2,1)S(1)} %pad_maximum_fusion.q_ref, bf16[128,4096]{1,0:T(8,128)(2,1)S(1)} %project_first.1.after_ref.also_ref, ...), custom_call_target="tpu_custom_call" | custom-call | flops 1 | bytes 1 | tf_op jit(solution)/shard_map/second_mine/pallas_call | solution.py:235
  101.9 3.0 %project_second.1.after_ref.also_ref = bf16[128,4096]{1,0:T(8,128)(2,1)S(1)} custom-call(s32[9]{0:T(128)S(1)} %pad_add_fusion.place, bf16[128,1024]{1,0:T(8,128)(2,1)S(1)} %second_mine.1.mine_ref.after_ref, bf16[128,1024]{1,0:T(8,128)(2,1)S(1)} %collective-permute-done.14.theirs_ref, bf16[2048,4096]{1,0:T(8,128)(2,1)S(1)} %hold_weight.1.after_ref.also_ref.held_ref, ...), custom_call_target="tpu_custom_call" | custom-call | flops 1 | bytes 1 | tf_op jit(solution)/shard_map/project_second/pallas_call | solution.py:304
  105.9 4.5 %own_theirs.1.after_ref.also_ref = bf16[128,1024]{1,0:T(8,128)(2,1)S(1)} custom-call(s32[1024]{0:T(1024)S(1)} %reshape.71.lists, s32[64]{0:T(128)S(1)} %reshape.72.counts, s32[9]{0:T(128)S(1)} %pad_add_fusion.place, bf16[2,8,512,128]{3,2,1,0:T(8,128)(2,1)S(1)} %pad_maximum_fusion.q_ref, bf16[128,4096]{1,0:T(8,128)(2,1)S(1)} %project_second.1.after_ref.also_ref, ...), custom_call_target="tpu_custom_call" | custom-call | flops 1 | bytes 1 | tf_op jit(solution)/shard_map/own_theirs/pallas_call | solution.py:235
  110.5 1.9 %collective-permute-start.15 = (bf16[128,1024]{1,0:T(8,128)(2,1)S(1)}, bf16[128,1024]{1,0:T(8,128)(2,1)S(1)}, u32[]{:S(2)}, u32[]{:S(2)}) collective-permute-start(bf16[128,1024]{1,0:T(8,128)(2,1)S(1)} %own_theirs.1.after_ref.also_ref), channel_id=1, source_target_pairs={{0,4},{4,0},{8,12},{12,8},{16,20},{20,16},{24,28},{28,24},{32,36},... | collective-permute-start | bytes 786440 | tf_op jit(solution)/shard_map/ppermute | solution.py:340
  112.4 4.5 %own_mine.1.mine_ref.after_ref = bf16[128,1024]{1,0:T(8,128)(2,1)S(1)} custom-call(s32[1024]{0:T(1024)S(1)} %reshape.71.lists, s32[64]{0:T(128)S(1)} %reshape.72.counts, s32[9]{0:T(128)S(1)} %pad_add_fusion.place, bf16[2,8,512,128]{3,2,1,0:T(8,128)(2,1)S(1)} %pad_maximum_fusion.q_ref, bf16[128,1024]{1,0:T(8,128)(2,1)S(1)} %own_theirs.1.after_ref.also_ref, ...), custom_call_target="tpu_custom_call" | custom-call | flops 1 | bytes 1 | tf_op jit(solution)/shard_map/own_mine/pallas_call | solution.py:235
  117.0 3.0 %project_own.1 = f32[128,4096]{1,0:T(8,128)S(1)} custom-call(s32[9]{0:T(128)S(1)} %pad_add_fusion.place, bf16[128,1024]{1,0:T(8,128)(2,1)S(1)} %own_mine.1.mine_ref.after_ref, bf16[128,1024]{1,0:T(8,128)(2,1)S(1)} %collective-permute-done.15.theirs_ref, bf16[2048,4096]{1,0:T(8,128)(2,1)S(1)} %hold_weight.1.after_ref.also_ref.held_ref, ...), custom_call_target="tpu_custom_call" | custom-call | flops 2000000000 | bytes 10000000 | tf_op jit(solution)/shard_map/project_own/pallas_call | solution.py:304
  120.0 3.4 %collective-permute-done.17 = bf16[128,4096]{1,0:T(8,128)(2,1)S(1)} collective-permute-done((bf16[128,4096]{1,0:T(8,128)(2,1)S(1)}, bf16[128,4096]{1,0:T(8,128)(2,1)S(1)}, u32[]{:S(2)}, u32[]{:S(2)}) %collective-permute-start.17) | collective-permute-done | bytes 1048608 | tf_op jit(solution)/shard_map/ppermute | solution.py:348
  123.4 1.2 add_convert_fusion
  (62 shorter events, 14.4 us)
Async XLA Ops:
  0.0 42.0 %copy-start = (s32[16,128,16]{1,2,0:T(8,128)S(1)}, s32[16,128,16]{1,2,0:T(8,128)}, u32[]{:S(2)}) copy-start(s32[16,128,16]{1,2,0:T(8,128)} %param.10) | copy-start | bytes 393220
  1.2 2.7 %collective-permute-start = (bf16[2,4,128,128]{3,2,1,0:T(8,128)(2,1)S(1)}, bf16[2,4,128,128]{3,2,1,0:T(8,128)(2,1)S(1)}, u32[]{:S(2)}, u32[]{:S(2)}) collective-permute-start(bf16[2,4,128,128]{3,2,1,0:T(8,128)(2,1)S(1)} %get-tuple-element.15), channel_id=1, source_target_pairs={{0,4},{4,0},{8,12},{12,8},{16,20},{20,16},{24,28},{28,24},{32,36},... | collective-permute-start | bytes 786440 | tf_op jit(solution)/shard_map/ppermute | solution.py:340
  3.9 10.7 %collective-permute-start.4 = (bf16[2,8,128,128]{3,2,1,0:T(8,128)(2,1)S(1)}, bf16[2,8,128,128]{3,2,1,0:T(8,128)(2,1)S(1)}, u32[]{:S(2)}, u32[]{:S(2)}) collective-permute-start(bf16[2,8,128,128]{3,2,1,0:T(8,128)(2,1)S(1)} %constant_dynamic-update-slice_fusion), channel_id=1, source_target_pairs={{0,16},{4,68},{8,24},{12,76},{16,0},{20,84},{24,8},{28,92},{32,48}... | collective-permute-start | bytes 1572872 | tf_op jit(solution)/shard_map/ppermute | solution.py:336
  7.7 13.1 %collective-permute-start.3 = (bf16[2,8,128,128]{3,2,1,0:T(8,128)(2,1)S(1)}, bf16[2,8,128,128]{3,2,1,0:T(8,128)(2,1)S(1)}, u32[]{:S(2)}, u32[]{:S(2)}) collective-permute-start(bf16[2,8,128,128]{3,2,1,0:T(8,128)(2,1)S(1)} %constant_dynamic-update-slice_fusion), channel_id=1, source_target_pairs={{0,24},{4,100},{8,0},{12,108},{16,8},{20,116},{24,16},{28,124},{32... | collective-permute-start | bytes 1572872 | tf_op jit(solution)/shard_map/ppermute | solution.py:336
  8.1 12.7 %collective-permute-start.1 = (bf16[2,8,128,128]{3,2,1,0:T(8,128)(2,1)S(1)}, bf16[2,8,128,128]{3,2,1,0:T(8,128)(2,1)S(1)}, u32[]{:S(2)}, u32[]{:S(2)}) collective-permute-start(bf16[2,8,128,128]{3,2,1,0:T(8,128)(2,1)S(1)} %constant_dynamic-update-slice_fusion), channel_id=1, source_target_pairs={{0,8},{4,36},{8,16},{12,44},{16,24},{20,52},{24,0},{28,60},{32,40}... | collective-permute-start | bytes 1572872 | tf_op jit(solution)/shard_map/ppermute | solution.py:336
  20.9 4.9 %copy-start.2 = (s32[1,4]{0,1:T(4,128)S(1)}, s32[1,4]{0,1:T(4,128)}, u32[]{:S(2)}) copy-start(s32[1,4]{0,1:T(4,128)} %constant.169) | copy-start | bytes 52
  20.9 4.9 %copy-start.3 = (s32[1,4]{0,1:T(4,128)S(1)}, s32[1,4]{0,1:T(4,128)}, u32[]{:S(2)}) copy-start(s32[1,4]{0,1:T(4,128)} %constant.168) | copy-start | bytes 52
  20.9 5.5 %copy-start.4 = (s32[16,128]{1,0:T(8,128)S(1)}, s32[16,128]{1,0:T(8,128)}, u32[]{:S(2)}) copy-start(s32[16,128]{1,0:T(8,128)} %param.11) | copy-start | bytes 24580
  22.0 15.5 %collective-permute-start.5 = (bf16[32,128,128]{2,1,0:T(8,128)(2,1)}, bf16[32,128,128]{2,1,0:T(8,128)(2,1)}, u32[]{:S(2)}, u32[]{:S(2)}) collective-permute-start(bf16[32,128,128]{2,1,0:T(8,128)(2,1)} %pad_maximum_fusion.1.refs_0_), channel_id=1, source_target_pairs={{0,32},{4,12},{8,40},{12,20},{16,48},{20,28},{24,56},{28,4},{32,64... | collective-permute-start | bytes 3145736 | tf_op jit(solution)/shard_map/ppermute | solution.py:336
  24.3 14.3 %collective-permute-start.7 = (bf16[32,128,128]{2,1,0:T(8,128)(2,1)}, bf16[32,128,128]{2,1,0:T(8,128)(2,1)}, u32[]{:S(2)}, u32[]{:S(2)}) collective-permute-start(bf16[32,128,128]{2,1,0:T(8,128)(2,1)} %pad_maximum_fusion.2.refs_3_), channel_id=1, source_target_pairs={{0,96},{4,28},{8,104},{12,4},{16,112},{20,12},{24,120},{28,20},{32... | collective-permute-start | bytes 3145736 | tf_op jit(solution)/shard_map/ppermute | solution.py:336
  26.6 23.2 %collective-permute-start.9 = (bf16[32,128,128]{2,1,0:T(8,128)(2,1)}, bf16[32,128,128]{2,1,0:T(8,128)(2,1)}, u32[]{:S(2)}, u32[]{:S(2)}) collective-permute-start(bf16[32,128,128]{2,1,0:T(8,128)(2,1)} %pad_maximum_fusion.1.refs_0_), channel_id=1, source_target_pairs={{0,96},{4,28},{8,104},{12,4},{16,112},{20,12},{24,120},{28,20},{32... | collective-permute-start | bytes 3145736 | tf_op jit(solution)/shard_map/ppermute | solution.py:336
  28.0 21.8 %collective-permute-start.10 = (bf16[32,128,128]{2,1,0:T(8,128)(2,1)}, bf16[32,128,128]{2,1,0:T(8,128)(2,1)}, u32[]{:S(2)}, u32[]{:S(2)}) collective-permute-start(bf16[32,128,128]{2,1,0:T(8,128)(2,1)} %pad_maximum_fusion.2.refs_3_), channel_id=1, source_target_pairs={{0,32},{4,12},{8,40},{12,20},{16,48},{20,28},{24,56},{28,4},{32,64... | collective-permute-start | bytes 3145736 | tf_op jit(solution)/shard_map/ppermute | solution.py:336
  30.1 22.5 %collective-permute-start.2 = (bf16[8,512,128]{2,1,0:T(8,128)(2,1)S(1)}, bf16[8,512,128]{2,1,0:T(8,128)(2,1)}, u32[]{:S(2)}, u32[]{:S(2)}) collective-permute-start(bf16[8,512,128]{2,1,0:T(8,128)(2,1)S(1)} %get-tuple-element.16), channel_id=1, source_target_pairs={{0,4},{4,0},{8,12},{12,8},{16,20},{20,16},{24,28},{28,24},{32,36},... | collective-permute-start | bytes 3145736 | tf_op jit(solution)/shard_map/ppermute | solution.py:340
  37.5 22.5 %collective-permute-start.6 = (bf16[32,128,128]{2,1,0:T(8,128)(2,1)}, bf16[32,128,128]{2,1,0:T(8,128)(2,1)}, u32[]{:S(2)}, u32[]{:S(2)}) collective-permute-start(bf16[32,128,128]{2,1,0:T(8,128)(2,1)} %collective-permute-done.5.refs_1_), channel_id=1, source_target_pairs={{0,32},{4,12},{8,40},{12,20},{16,48},{20,28},{24,56},{28,4},{32,64... | collective-permute-start | bytes 3145736 | tf_op jit(solution)/shard_map/ppermute | solution.py:336
  38.6 22.5 %collective-permute-start.8 = (bf16[32,128,128]{2,1,0:T(8,128)(2,1)}, bf16[32,128,128]{2,1,0:T(8,128)(2,1)}, u32[]{:S(2)}, u32[]{:S(2)}) collective-permute-start(bf16[32,128,128]{2,1,0:T(8,128)(2,1)} %collective-permute-done.7.refs_5_), channel_id=1, source_target_pairs={{0,96},{4,28},{8,104},{12,4},{16,112},{20,12},{24,120},{28,20},{32... | collective-permute-start | bytes 3145736 | tf_op jit(solution)/shard_map/ppermute | solution.py:336
  66.8 6.6 %collective-permute-start.11 = (bf16[128,1024]{1,0:T(8,128)(2,1)S(1)}, bf16[128,1024]{1,0:T(8,128)(2,1)S(1)}, u32[]{:S(2)}, u32[]{:S(2)}) collective-permute-start(bf16[128,1024]{1,0:T(8,128)(2,1)S(1)} %get-tuple-element.20.after_ref.also_ref), channel_id=1, source_target_pairs={{0,4},{4,0},{8,12},{12,8},{16,20},{20,16},{24,28},{28,24},{32,36},... | collective-permute-start | bytes 786440 | tf_op jit(solution)/shard_map/ppermute | solution.py:340
  76.5 17.0 %collective-permute-start.13 = (bf16[128,4096]{1,0:T(8,128)(2,1)S(1)}, bf16[128,4096]{1,0:T(8,128)(2,1)S(1)}, u32[]{:S(2)}, u32[]{:S(2)}) collective-permute-start(bf16[128,4096]{1,0:T(8,128)(2,1)S(1)} %project_far.1.after_ref.also_ref), channel_id=1, source_target_pairs={{0,1},{1,2},{2,3},{3,0},{4,7},{5,4},{6,5},{7,6},{8,9},{9,10},{10,1... | collective-permute-start | bytes 3145736 | tf_op jit(solution)/shard_map/ppermute | solution.py:348
  83.8 9.8 %collective-permute-start.12 = (bf16[128,1024]{1,0:T(8,128)(2,1)S(1)}, bf16[128,1024]{1,0:T(8,128)(2,1)S(1)}, u32[]{:S(2)}, u32[]{:S(2)}) collective-permute-start(bf16[128,1024]{1,0:T(8,128)(2,1)S(1)} %first_theirs.1.after_ref.also_ref), channel_id=1, source_target_pairs={{0,4},{4,0},{8,12},{12,8},{16,20},{20,16},{24,28},{28,24},{32,36},... | collective-permute-start | bytes 786440 | tf_op jit(solution)/shard_map/ppermute | solution.py:340
  93.0 8.9 %collective-permute-start.14 = (bf16[128,1024]{1,0:T(8,128)(2,1)S(1)}, bf16[128,1024]{1,0:T(8,128)(2,1)S(1)}, u32[]{:S(2)}, u32[]{:S(2)}) collective-permute-start(bf16[128,1024]{1,0:T(8,128)(2,1)S(1)} %second_theirs.1.after_ref), channel_id=1, source_target_pairs={{0,4},{4,0},{8,12},{12,8},{16,20},{20,16},{24,28},{28,24},{32,36},... | collective-permute-start | bytes 786440 | tf_op jit(solution)/shard_map/ppermute | solution.py:340
  96.5 20.4 %collective-permute-start.16 = (bf16[128,4096]{1,0:T(8,128)(2,1)S(1)}, bf16[128,4096]{1,0:T(8,128)(2,1)S(1)}, u32[]{:S(2)}, u32[]{:S(2)}) collective-permute-start(bf16[128,4096]{1,0:T(8,128)(2,1)S(1)} %project_first.1.after_ref.also_ref), channel_id=1, source_target_pairs={{0,1},{1,2},{2,3},{3,0},{4,7},{5,4},{6,5},{7,6},{8,9},{9,10},{10,1... | collective-permute-start | bytes 3145736 | tf_op jit(solution)/shard_map/ppermute | solution.py:348
  104.9 18.5 %collective-permute-start.17 = (bf16[128,4096]{1,0:T(8,128)(2,1)S(1)}, bf16[128,4096]{1,0:T(8,128)(2,1)S(1)}, u32[]{:S(2)}, u32[]{:S(2)}) collective-permute-start(bf16[128,4096]{1,0:T(8,128)(2,1)S(1)} %project_second.1.after_ref.also_ref), channel_id=1, source_target_pairs={{0,3},{1,0},{2,1},{3,2},{4,5},{5,6},{6,7},{7,4},{8,11},{9,8},{10,9... | collective-permute-start | bytes 3145736 | tf_op jit(solution)/shard_map/ppermute | solution.py:348
  110.5 6.5 %collective-permute-start.15 = (bf16[128,1024]{1,0:T(8,128)(2,1)S(1)}, bf16[128,1024]{1,0:T(8,128)(2,1)S(1)}, u32[]{:S(2)}, u32[]{:S(2)}) collective-permute-start(bf16[128,1024]{1,0:T(8,128)(2,1)S(1)} %own_theirs.1.after_ref.also_ref), channel_id=1, source_target_pairs={{0,4},{4,0},{8,12},{12,8},{16,20},{20,16},{24,28},{28,24},{32,36},... | collective-permute-start | bytes 786440 | tf_op jit(solution)/shard_map/ppermute | solution.py:340
  117.0 7.7 %copy-start.1 = (s32[16,128,16]{1,2,0:T(8,128)S(1)}, s32[16,128,16]{1,2,0:T(8,128)}, u32[]{:S(2)}) copy-start(s32[16,128,16]{1,2,0:T(8,128)} %param.10) | copy-start | bytes 393220
where the time goes:
time: 125 us
  Pallas kernels  61.6 us (49%)
  waiting for transfers between devices  30 us (24%)
  starting transfers between devices  25.1 us (20%)
  other arithmetic  5.44 us (4%)
  local copies, waits for them, and re-layouts  2.19 us (2%)
    pallas_call x8, Pallas kernels, attend_call(): pl.pallas_call(functools.partial(attend_kernel, chunk * CHUNK_COUPLES + s...  37.6 us
    ppermute x9, waiting for transfers between devices, along(): return lax.ppermute(array, 'seq', chip_perm(phase, step))  25.4 us
    ppermute x9, starting transfers between devices, along(): return lax.ppermute(array, 'seq', chip_perm(phase, step))  12.1 us
    pallas_call x4, Pallas kernels, project_call(): pl.pallas_call(functools.partial(project_kernel, kind), name='project_' +...  12 us
    ppermute x6, starting transfers between devices, swap(): return lax.ppermute(array, 'seq', SWAP)  8.51 us
    pallas_call x1, Pallas kernels, hold_call(): pl.pallas_call(hold_kernel, name='hold_weight', in_specs=[HBM, HBM], out_...  5.78 us
    ppermute x3, starting transfers between devices, turn(): return lax.ppermute(array, ('seq', 'grp'), pairs)  4.55 us
    ppermute x3, waiting for transfers between devices, turn(): return lax.ppermute(array, ('seq', 'grp'), pairs)  3.45 us
  transfers between devices with their start and end apart: 18, of which 9 were waited for; matrix products, arithmetic and copies ran while one was open for 4% of the time, Pallas kernels for 41%

commit v1 on v0

--- a/solution.py
+++ b/solution.py
@@ -293,7 +293,7 @@
     for at in range(0, width, tile):
         cols = slice(at, at + tile)
         total = jnp.dot(both, held_ref[:, cols], preferred_element_type=jnp.float32)
-        if kind in ("first", "own"):
+        if kind in ("last", "own"):
             total = total + refs[0][:, cols].astype(jnp.float32)
         out_ref[:, cols] = total.astype(out_ref.dtype)
 
@@ -374,7 +374,7 @@
     chip = seq_place // CORES
     chip_z, chip_y = chip // RING, chip % RING
 
-    ways = jnp.array([[2, 1, 3, 0], [2, 3, 1, 0]], jnp.int32)
+    ways = jnp.array([[2, 3, 1, 0], [2, 1, 3, 0]], jnp.int32)
     mine_chunks = jnp.where(core == 0, ways[0], ways[1])
     theirs_chunks = jnp.where(core == 0, ways[1], ways[0])
     chunks = (grp_place + jnp.stack([theirs_chunks, mine_chunks])) % RING
@@ -425,19 +425,15 @@
     far_mine = attend("far_mine", 0, 1, (far_theirs, far_theirs))
     far = project_call("far", place, far_mine, swap(far_theirs), held, far_mine)
     passed = turn(far, 1)
-    first_theirs = attend("first_theirs", 1, 0, (far, far))
-    first_mine = attend("first_mine", 1, 1, (first_theirs, first_theirs))
-    second_theirs = attend("second_theirs", 2, 0, (first_mine, first_mine))
-    first = project_call(
-        "first", place, first_mine, swap(first_theirs), held, second_theirs, passed
-    )
-    arrived = turn(first, 1)
-    second_mine = attend("second_mine", 2, 1, (first, first))
-    second = project_call(
-        "second", place, second_mine, swap(second_theirs), held, second_mine
-    )
-    arrived_last = turn(second, -1)
-    own_theirs = attend("own_theirs", 3, 0, (second, second))
+    near_theirs = attend("near_theirs", 1, 0, (far, far))
+    near_mine = attend("near_mine", 1, 1, (near_theirs, near_theirs))
+    near = project_call("near", place, near_mine, swap(near_theirs), held, near_mine)
+    arrived = turn(near, -1)
+    last_theirs = attend("last_theirs", 2, 0, (near, near))
+    last_mine = attend("last_mine", 2, 1, (last_theirs, last_theirs))
+    last = project_call("last", place, last_mine, swap(last_theirs), held, last_mine, passed)
+    arrived_last = turn(last, 1)
+    own_theirs = attend("own_theirs", 3, 0, (last, arrived))
     own_mine = attend("own_mine", 3, 1, (own_theirs, own_theirs))
     own = project_call("own", place, own_mine, swap(own_theirs), held, own_mine, arrived)
     total = own + arrived_last.astype(jnp.float32)

time: 125 us -> 121 us (0.968)
  waiting for transfers between devices: 30 us -> 26.7 us
    ppermute x3, waiting for transfers between devices: 3.45 us -> 0.21 us  [turn(): return lax.ppermute(array, ('seq', 'grp'), pairs)]
  transfers between devices with their start and end apart: 18 -> 18, of which waited for: 9 -> 9; matrix products, arithmetic and copies ran while one was open for 4% -> 4% of each run, Pallas kernels for 41% -> 43%
where the time goes in v1:
time: 121 us; the launch traced here: 120 us
  Pallas kernels  61.4 us (51%)
  waiting for transfers between devices  26.7 us (22%)
  starting transfers between devices  24.2 us (20%)
  other arithmetic  5.44 us (4%)
  local copies, waits for them, and re-layouts  2.19 us (2%)
    pallas_call x8, Pallas kernels, attend_call(): pl.pallas_call(functools.partial(attend_kernel, chunk * CHUNK_COUPLES + s...  37.6 us
    ppermute x9, waiting for transfers between devices, along(): return lax.ppermute(array, 'seq', chip_perm(phase, step))  25.4 us
    ppermute x9, starting transfers between devices, along(): return lax.ppermute(array, 'seq', chip_perm(phase, step))  12.1 us
    pallas_call x4, Pallas kernels, project_call(): pl.pallas_call(functools.partial(project_kernel, kind), name='project_' +...  11.9 us
    ppermute x6, starting transfers between devices, swap(): return lax.ppermute(array, 'seq', SWAP)  7.69 us
    pallas_call x1, Pallas kernels, hold_call(): pl.pallas_call(hold_kernel, name='hold_weight', in_specs=[HBM, HBM], out_...  5.78 us
    ppermute x3, starting transfers between devices, turn(): return lax.ppermute(array, ('seq', 'grp'), pairs)  4.46 us
    pallas_call x1, Pallas kernels, tables_call(): pl.pallas_call(functools.partial(tables_kernel, places), name='tables', i...  2.85 us
  transfers between devices with their start and end apart: 18, of which 9 were waited for; matrix products, arithmetic and copies ran while one was open for 4% of the time, Pallas kernels for 43%

profile of v1, /device:TPU:1, one launch (start us, length us, event | category | flops | bytes accessed | tf_op | source)
XLA Modules:
  0.0 120.4 jit_solution(2613423220800682220)
XLA Ops:
  0.0 1.2 %prepare.1 = (bf16[2,4,128,128]{3,2,1,0:T(8,128)(2,1)S(1)}, bf16[2,4,128,128]{3,2,1,0:T(8,128)(2,1)S(1)}) custom-call(bf16[2,512,128]{2,1,0:T(8,128)(2,1)} %key_ref.1, bf16[2,512,128]{2,1,0:T(8,128)(2,1)} %value_ref.1), custom_call_target="tpu_custom_call" | custom-call | flops 1 | bytes 1 | tf_op jit(solution)/shard_map/prepare/pallas_call | solution.py:159
  1.2 1.5 %collective-permute-start = (bf16[2,4,128,128]{3,2,1,0:T(8,128)(2,1)S(1)}, bf16[2,4,128,128]{3,2,1,0:T(8,128)(2,1)S(1)}, u32[]{:S(2)}, u32[]{:S(2)}) collective-permute-start(bf16[2,4,128,128]{3,2,1,0:T(8,128)(2,1)S(1)} %get-tuple-element.15), channel_id=1, source_target_pairs={{0,4},{4,0},{8,12},{12,8},{16,20},{20,16},{24,28},{28,24},{32,36},... | collective-permute-start | bytes 786440 | tf_op jit(solution)/shard_map/ppermute | solution.py:340
  3.9 3.8 %collective-permute-start.4 = (bf16[2,8,128,128]{3,2,1,0:T(8,128)(2,1)S(1)}, bf16[2,8,128,128]{3,2,1,0:T(8,128)(2,1)S(1)}, u32[]{:S(2)}, u32[]{:S(2)}) collective-permute-start(bf16[2,8,128,128]{3,2,1,0:T(8,128)(2,1)S(1)} %constant_dynamic-update-slice_fusion), channel_id=1, source_target_pairs={{0,16},{4,68},{8,24},{12,76},{16,0},{20,84},{24,8},{28,92},{32,48}... | collective-permute-start | bytes 1572872 | tf_op jit(solution)/shard_map/ppermute | solution.py:336
  9.2 5.4 %collective-permute-done.4 = bf16[2,8,128,128]{3,2,1,0:T(8,128)(2,1)S(1)} collective-permute-done((bf16[2,8,128,128]{3,2,1,0:T(8,128)(2,1)S(1)}, bf16[2,8,128,128]{3,2,1,0:T(8,128)(2,1)S(1)}, u32[]{:S(2)}, u32[]{:S(2)}) %collective-permute-start.4) | collective-permute-done | bytes 524320 | tf_op jit(solution)/shard_map/ppermute | solution.py:336
  14.6 6.1 %collective-permute-done.3 = bf16[2,8,128,128]{3,2,1,0:T(8,128)(2,1)S(1)} collective-permute-done((bf16[2,8,128,128]{3,2,1,0:T(8,128)(2,1)S(1)}, bf16[2,8,128,128]{3,2,1,0:T(8,128)(2,1)S(1)}, u32[]{:S(2)}, u32[]{:S(2)}) %collective-permute-start.3) | collective-permute-done | bytes 524320 | tf_op jit(solution)/shard_map/ppermute | solution.py:336
  24.3 1.5 %collective-permute-start.7 = (bf16[32,128,128]{2,1,0:T(8,128)(2,1)}, bf16[32,128,128]{2,1,0:T(8,128)(2,1)}, u32[]{:S(2)}, u32[]{:S(2)}) collective-permute-start(bf16[32,128,128]{2,1,0:T(8,128)(2,1)} %pad_maximum_fusion.2.refs_3_), channel_id=1, source_target_pairs={{0,96},{4,28},{8,104},{12,4},{16,112},{20,12},{24,120},{28,20},{32... | collective-permute-start | bytes 3145736 | tf_op jit(solution)/shard_map/ppermute | solution.py:336
  26.6 1.4 %collective-permute-start.9 = (bf16[32,128,128]{2,1,0:T(8,128)(2,1)}, bf16[32,128,128]{2,1,0:T(8,128)(2,1)}, u32[]{:S(2)}, u32[]{:S(2)}) collective-permute-start(bf16[32,128,128]{2,1,0:T(8,128)(2,1)} %pad_maximum_fusion.1.refs_0_), channel_id=1, source_target_pairs={{0,96},{4,28},{8,104},{12,4},{16,112},{20,12},{24,120},{28,20},{32... | collective-permute-start | bytes 3145736 | tf_op jit(solution)/shard_map/ppermute | solution.py:336
  28.0 2.1 %queries.1 = (bf16[8,512,128]{2,1,0:T(8,128)(2,1)S(1)}, bf16[8,512,128]{2,1,0:T(8,128)(2,1)S(1)}) custom-call(s32[9]{0:T(128)S(1)} %pad_add_fusion.place, bf16[16,512,128]{2,1,0:T(8,128)(2,1)} %source_ref.2, bf16[2,8,128,128]{3,2,1,0:T(8,128)(2,1)S(1)} %collective-permute-done.1.after_ref), custom_call_target="tpu_custom_call" | custom-call | flops 1 | bytes 1 | tf_op jit(solution)/shard_map/queries/pallas_call | solution.py:269
  30.1 2.4 %collective-permute-start.2 = (bf16[8,512,128]{2,1,0:T(8,128)(2,1)S(1)}, bf16[8,512,128]{2,1,0:T(8,128)(2,1)}, u32[]{:S(2)}, u32[]{:S(2)}) collective-permute-start(bf16[8,512,128]{2,1,0:T(8,128)(2,1)S(1)} %get-tuple-element.16), channel_id=1, source_target_pairs={{0,4},{4,0},{8,12},{12,8},{16,20},{20,16},{24,28},{28,24},{32,36},... | collective-permute-start | bytes 3145736 | tf_op jit(solution)/shard_map/ppermute | solution.py:340
  32.5 4.9 %collective-permute-done.5.refs_1_ = bf16[32,128,128]{2,1,0:T(8,128)(2,1)} collective-permute-done((bf16[32,128,128]{2,1,0:T(8,128)(2,1)}, bf16[32,128,128]{2,1,0:T(8,128)(2,1)}, u32[]{:S(2)}, u32[]{:S(2)}) %collective-permute-start.5) | collective-permute-done | bytes 1048608 | tf_op jit(solution)/shard_map/ppermute | solution.py:336
  38.6 2.7 %collective-permute-start.8 = (bf16[32,128,128]{2,1,0:T(8,128)(2,1)}, bf16[32,128,128]{2,1,0:T(8,128)(2,1)}, u32[]{:S(2)}, u32[]{:S(2)}) collective-permute-start(bf16[32,128,128]{2,1,0:T(8,128)(2,1)} %collective-permute-done.7.refs_5_), channel_id=1, source_target_pairs={{0,96},{4,28},{8,104},{12,4},{16,112},{20,12},{24,120},{28,20},{32... | collective-permute-start | bytes 3145736 | tf_op jit(solution)/shard_map/ppermute | solution.py:336
  43.1 5.8 %hold_weight.1.after_ref.also_ref.held_ref = bf16[2048,4096]{1,0:T(8,128)(2,1)S(1)} custom-call(bf16[2048,4096]{1,0:T(8,128)(2,1)} %source_ref.3, bf16[2,8,128,128]{3,2,1,0:T(8,128)(2,1)S(1)} %collective-permute-done.1.after_ref), custom_call_target="tpu_custom_call" | custom-call | tf_op jit(solution)/shard_map/hold_weight/pallas_call | solution.py:128
  49.8 2.9 %tables.1 = (bf16[128,128,128]{2,1,0:T(8,128)(2,1)S(1)}, bf16[128,128,128]{2,1,0:T(8,128)(2,1)S(1)}) custom-call(bf16[32,128,128]{2,1,0:T(8,128)(2,1)} %pad_maximum_fusion.1.refs_0_, bf16[32,128,128]{2,1,0:T(8,128)(2,1)} %collective-permute-done.5.refs_1_, bf16[32,128,128]{2,1,0:T(8,128)(2,1)} %collective-permute-done.9.refs_2_, ...), custom_call_target="tpu_custom_call" | custom-call | flops 1 | bytes 1 | tf_op jit(solution)/shard_map/tables/pallas_call | solution.py:192
  52.7 1.4 %pad_maximum_fusion.q_ref = bf16[2,8,512,128]{3,2,1,0:T(8,128)(2,1)S(1)} fusion(bf16[1,8,512,128]{3,2,1,0:T(8,128)(2,1)S(1)} %bitcast.24, bf16[1,8,512,128]{3,2,1,0:T(8,128)(2,1)} %bitcast.4), kind=kLoop, calls=%fused_computation.2 | loop fusion | flops 1048576 | bytes 4194304 | tf_op jit(solution)/shard_map/stack | solution.py:386
  54.1 5.8 %collective-permute-done.6.refs_0_ = bf16[32,128,128]{2,1,0:T(8,128)(2,1)} collective-permute-done((bf16[32,128,128]{2,1,0:T(8,128)(2,1)}, bf16[32,128,128]{2,1,0:T(8,128)(2,1)}, u32[]{:S(2)}, u32[]{:S(2)}) %collective-permute-start.6) | collective-permute-done | bytes 1048608 | tf_op jit(solution)/shard_map/ppermute | solution.py:336
  61.0 5.8 %far_theirs.1 = (bf16[128,1024]{1,0:T(8,128)(2,1)S(1)}, bf16[128,128,128]{2,1,0:T(8,128)(2,1)S(1)}, bf16[128,128,128]{2,1,0:T(8,128)(2,1)S(1)}) custom-call(s32[1024]{0:T(1024)S(1)} %reshape.71.lists, s32[64]{0:T(128)S(1)} %reshape.72.counts, s32[9]{0:T(128)S(1)} %pad_add_fusion.place, ...), custom_call_target="tpu_custom_call", output_to_operand_aliasing={{1}: (8, {}), {2}: (9, {})} | custom-call | flops 1 | bytes 1 | tf_op jit(solution)/shard_map/far_theirs/pallas_call | solution.py:235
  66.8 2.1 %collective-permute-start.11 = (bf16[128,1024]{1,0:T(8,128)(2,1)S(1)}, bf16[128,1024]{1,0:T(8,128)(2,1)S(1)}, u32[]{:S(2)}, u32[]{:S(2)}) collective-permute-start(bf16[128,1024]{1,0:T(8,128)(2,1)S(1)} %get-tuple-element.20.after_ref.also_ref), channel_id=1, source_target_pairs={{0,4},{4,0},{8,12},{12,8},{16,20},{20,16},{24,28},{28,24},{32,36},... | collective-permute-start | bytes 786440 | tf_op jit(solution)/shard_map/ppermute | solution.py:340
  68.9 4.5 %far_mine.1.mine_ref.after_ref = bf16[128,1024]{1,0:T(8,128)(2,1)S(1)} custom-call(s32[1024]{0:T(1024)S(1)} %reshape.71.lists, s32[64]{0:T(128)S(1)} %reshape.72.counts, s32[9]{0:T(128)S(1)} %pad_add_fusion.place, bf16[2,8,512,128]{3,2,1,0:T(8,128)(2,1)S(1)} %pad_maximum_fusion.q_ref, bf16[128,1024]{1,0:T(8,128)(2,1)S(1)} %get-tuple-element.20.after_ref.also_ref, ...), custom_call_target="tpu_custom_call" | custom-call | flops 1 | bytes 1 | tf_op jit(solution)/shard_map/far_mine/pallas_call | solution.py:235
  73.5 3.0 %project_far.1.after_ref.also_ref = bf16[128,4096]{1,0:T(8,128)(2,1)S(1)} custom-call(s32[9]{0:T(128)S(1)} %pad_add_fusion.place, bf16[128,1024]{1,0:T(8,128)(2,1)S(1)} %far_mine.1.mine_ref.after_ref, bf16[128,1024]{1,0:T(8,128)(2,1)S(1)} %collective-permute-done.11.theirs_ref, bf16[2048,4096]{1,0:T(8,128)(2,1)S(1)} %hold_weight.1.after_ref.also_ref.held_ref, ...), custom_call_target="tpu_custom_call" | custom-call | flops 1 | bytes 1 | tf_op jit(solution)/shard_map/project_far/pallas_call | solution.py:304
  76.5 2.7 %collective-permute-start.14 = (bf16[128,4096]{1,0:T(8,128)(2,1)S(1)}, bf16[128,4096]{1,0:T(8,128)(2,1)S(1)}, u32[]{:S(2)}, u32[]{:S(2)}) collective-permute-start(bf16[128,4096]{1,0:T(8,128)(2,1)S(1)} %project_far.1.after_ref.also_ref), channel_id=1, source_target_pairs={{0,1},{1,2},{2,3},{3,0},{4,7},{5,4},{6,5},{7,6},{8,9},{9,10},{10,1... | collective-permute-start | bytes 3145736 | tf_op jit(solution)/shard_map/ppermute | solution.py:348
  79.2 4.5 %near_theirs.1.after_ref.also_ref = bf16[128,1024]{1,0:T(8,128)(2,1)S(1)} custom-call(s32[1024]{0:T(1024)S(1)} %reshape.71.lists, s32[64]{0:T(128)S(1)} %reshape.72.counts, s32[9]{0:T(128)S(1)} %pad_add_fusion.place, bf16[2,8,512,128]{3,2,1,0:T(8,128)(2,1)S(1)} %pad_maximum_fusion.q_ref, bf16[128,4096]{1,0:T(8,128)(2,1)S(1)} %project_far.1.after_ref.also_ref, ...), custom_call_target="tpu_custom_call" | custom-call | flops 1 | bytes 1 | tf_op jit(solution)/shard_map/near_theirs/pallas_call | solution.py:235
  83.9 4.5 %near_mine.1.mine_ref.after_ref = bf16[128,1024]{1,0:T(8,128)(2,1)S(1)} custom-call(s32[1024]{0:T(1024)S(1)} %reshape.71.lists, s32[64]{0:T(128)S(1)} %reshape.72.counts, s32[9]{0:T(128)S(1)} %pad_add_fusion.place, bf16[2,8,512,128]{3,2,1,0:T(8,128)(2,1)S(1)} %pad_maximum_fusion.q_ref, bf16[128,1024]{1,0:T(8,128)(2,1)S(1)} %near_theirs.1.after_ref.also_ref, ...), custom_call_target="tpu_custom_call" | custom-call | flops 1 | bytes 1 | tf_op jit(solution)/shard_map/near_mine/pallas_call | solution.py:235
  88.4 3.0 %project_near.1.after_ref.also_ref = bf16[128,4096]{1,0:T(8,128)(2,1)S(1)} custom-call(s32[9]{0:T(128)S(1)} %pad_add_fusion.place, bf16[128,1024]{1,0:T(8,128)(2,1)S(1)} %near_mine.1.mine_ref.after_ref, bf16[128,1024]{1,0:T(8,128)(2,1)S(1)} %collective-permute-done.12.theirs_ref, bf16[2048,4096]{1,0:T(8,128)(2,1)S(1)} %hold_weight.1.after_ref.also_ref.held_ref, ...), custom_call_target="tpu_custom_call" | custom-call | flops 1 | bytes 1 | tf_op jit(solution)/shard_map/project_near/pallas_call | solution.py:304
  91.7 4.5 %last_theirs.1.after_ref.also_ref = bf16[128,1024]{1,0:T(8,128)(2,1)S(1)} custom-call(s32[1024]{0:T(1024)S(1)} %reshape.71.lists, s32[64]{0:T(128)S(1)} %reshape.72.counts, s32[9]{0:T(128)S(1)} %pad_add_fusion.place, bf16[2,8,512,128]{3,2,1,0:T(8,128)(2,1)S(1)} %pad_maximum_fusion.q_ref, bf16[128,4096]{1,0:T(8,128)(2,1)S(1)} %project_near.1.after_ref.also_ref, ...), custom_call_target="tpu_custom_call" | custom-call | flops 1 | bytes 1 | tf_op jit(solution)/shard_map/last_theirs/pallas_call | solution.py:235
  96.2 1.4 %collective-permute-start.13 = (bf16[128,1024]{1,0:T(8,128)(2,1)S(1)}, bf16[128,1024]{1,0:T(8,128)(2,1)S(1)}, u32[]{:S(2)}, u32[]{:S(2)}) collective-permute-start(bf16[128,1024]{1,0:T(8,128)(2,1)S(1)} %last_theirs.1.after_ref.also_ref), channel_id=1, source_target_pairs={{0,4},{4,0},{8,12},{12,8},{16,20},{20,16},{24,28},{28,24},{32,36},... | collective-permute-start | bytes 786440 | tf_op jit(solution)/shard_map/ppermute | solution.py:340
  97.6 4.5 %last_mine.1.mine_ref.after_ref = bf16[128,1024]{1,0:T(8,128)(2,1)S(1)} custom-call(s32[1024]{0:T(1024)S(1)} %reshape.71.lists, s32[64]{0:T(128)S(1)} %reshape.72.counts, s32[9]{0:T(128)S(1)} %pad_add_fusion.place, bf16[2,8,512,128]{3,2,1,0:T(8,128)(2,1)S(1)} %pad_maximum_fusion.q_ref, bf16[128,1024]{1,0:T(8,128)(2,1)S(1)} %last_theirs.1.after_ref.also_ref, ...), custom_call_target="tpu_custom_call" | custom-call | flops 1 | bytes 1 | tf_op jit(solution)/shard_map/last_mine/pallas_call | solution.py:235
  102.2 2.9 %project_last.1.after_ref = bf16[128,4096]{1,0:T(8,128)(2,1)S(1)} custom-call(s32[9]{0:T(128)S(1)} %pad_add_fusion.place, bf16[128,1024]{1,0:T(8,128)(2,1)S(1)} %last_mine.1.mine_ref.after_ref, bf16[128,1024]{1,0:T(8,128)(2,1)S(1)} %collective-permute-done.13.theirs_ref, bf16[2048,4096]{1,0:T(8,128)(2,1)S(1)} %hold_weight.1.after_ref.also_ref.held_ref, ...), custom_call_target="tpu_custom_call" | custom-call | flops 1 | bytes 1 | tf_op jit(solution)/shard_map/project_last/pallas_call | solution.py:304
  105.2 1.5 %collective-permute-start.17 = (bf16[128,4096]{1,0:T(8,128)(2,1)S(1)}, bf16[128,4096]{1,0:T(8,128)(2,1)S(1)}, u32[]{:S(2)}, u32[]{:S(2)}) collective-permute-start(bf16[128,4096]{1,0:T(8,128)(2,1)S(1)} %project_last.1.after_ref), channel_id=1, source_target_pairs={{0,1},{1,2},{2,3},{3,0},{4,7},{5,4},{6,5},{7,6},{8,9},{9,10},{10,1... | collective-permute-start | bytes 3145736 | tf_op jit(solution)/shard_map/ppermute | solution.py:348
  106.6 4.5 %own_theirs.1.after_ref.also_ref = bf16[128,1024]{1,0:T(8,128)(2,1)S(1)} custom-call(s32[1024]{0:T(1024)S(1)} %reshape.71.lists, s32[64]{0:T(128)S(1)} %reshape.72.counts, s32[9]{0:T(128)S(1)} %pad_add_fusion.place, bf16[2,8,512,128]{3,2,1,0:T(8,128)(2,1)S(1)} %pad_maximum_fusion.q_ref, bf16[128,4096]{1,0:T(8,128)(2,1)S(1)} %project_last.1.after_ref, ...), custom_call_target="tpu_custom_call" | custom-call | flops 1 | bytes 1 | tf_op jit(solution)/shard_map/own_theirs/pallas_call | solution.py:235
  111.4 4.5 %own_mine.1.mine_ref.after_ref = bf16[128,1024]{1,0:T(8,128)(2,1)S(1)} custom-call(s32[1024]{0:T(1024)S(1)} %reshape.71.lists, s32[64]{0:T(128)S(1)} %reshape.72.counts, s32[9]{0:T(128)S(1)} %pad_add_fusion.place, bf16[2,8,512,128]{3,2,1,0:T(8,128)(2,1)S(1)} %pad_maximum_fusion.q_ref, bf16[128,1024]{1,0:T(8,128)(2,1)S(1)} %own_theirs.1.after_ref.also_ref, ...), custom_call_target="tpu_custom_call" | custom-call | flops 1 | bytes 1 | tf_op jit(solution)/shard_map/own_mine/pallas_call | solution.py:235
  116.0 3.0 %project_own.1 = f32[128,4096]{1,0:T(8,128)S(1)} custom-call(s32[9]{0:T(128)S(1)} %pad_add_fusion.place, bf16[128,1024]{1,0:T(8,128)(2,1)S(1)} %own_mine.1.mine_ref.after_ref, bf16[128,1024]{1,0:T(8,128)(2,1)S(1)} %collective-permute-done.16.theirs_ref, bf16[2048,4096]{1,0:T(8,128)(2,1)S(1)} %hold_weight.1.after_ref.also_ref.held_ref, ...), custom_call_target="tpu_custom_call" | custom-call | flops 2000000000 | bytes 10000000 | tf_op jit(solution)/shard_map/project_own/pallas_call | solution.py:304
  119.2 1.2 %add_convert_fusion = bf16[128,4096]{1,0:T(8,128)(2,1)} fusion(f32[128,4096]{1,0:T(8,128)S(1)} %project_own.1, bf16[128,4096]{1,0:T(8,128)(2,1)S(1)} %collective-permute-done.17), kind=kLoop, calls=%fused_computation.3 | loop fusion | flops 1572864 | bytes 4194304 | tf_op jit(solution)/shard_map/convert_element_type | solution.py:440
  (62 shorter events, 12.7 us)
Async XLA Ops:
  0.0 42.0 %copy-start = (s32[16,128,16]{1,2,0:T(8,128)S(1)}, s32[16,128,16]{1,2,0:T(8,128)}, u32[]{:S(2)}) copy-start(s32[16,128,16]{1,2,0:T(8,128)} %param.10) | copy-start | bytes 393220
  1.2 2.7 %collective-permute-start = (bf16[2,4,128,128]{3,2,1,0:T(8,128)(2,1)S(1)}, bf16[2,4,128,128]{3,2,1,0:T(8,128)(2,1)S(1)}, u32[]{:S(2)}, u32[]{:S(2)}) collective-permute-start(bf16[2,4,128,128]{3,2,1,0:T(8,128)(2,1)S(1)} %get-tuple-element.15), channel_id=1, source_target_pairs={{0,4},{4,0},{8,12},{12,8},{16,20},{20,16},{24,28},{28,24},{32,36},... | collective-permute-start | bytes 786440 | tf_op jit(solution)/shard_map/ppermute | solution.py:340
  3.9 10.7 %collective-permute-start.4 = (bf16[2,8,128,128]{3,2,1,0:T(8,128)(2,1)S(1)}, bf16[2,8,128,128]{3,2,1,0:T(8,128)(2,1)S(1)}, u32[]{:S(2)}, u32[]{:S(2)}) collective-permute-start(bf16[2,8,128,128]{3,2,1,0:T(8,128)(2,1)S(1)} %constant_dynamic-update-slice_fusion), channel_id=1, source_target_pairs={{0,16},{4,68},{8,24},{12,76},{16,0},{20,84},{24,8},{28,92},{32,48}... | collective-permute-start | bytes 1572872 | tf_op jit(solution)/shard_map/ppermute | solution.py:336
  7.7 13.1 %collective-permute-start.3 = (bf16[2,8,128,128]{3,2,1,0:T(8,128)(2,1)S(1)}, bf16[2,8,128,128]{3,2,1,0:T(8,128)(2,1)S(1)}, u32[]{:S(2)}, u32[]{:S(2)}) collective-permute-start(bf16[2,8,128,128]{3,2,1,0:T(8,128)(2,1)S(1)} %constant_dynamic-update-slice_fusion), channel_id=1, source_target_pairs={{0,24},{4,100},{8,0},{12,108},{16,8},{20,116},{24,16},{28,124},{32... | collective-permute-start | bytes 1572872 | tf_op jit(solution)/shard_map/ppermute | solution.py:336
  8.1 12.7 %collective-permute-start.1 = (bf16[2,8,128,128]{3,2,1,0:T(8,128)(2,1)S(1)}, bf16[2,8,128,128]{3,2,1,0:T(8,128)(2,1)S(1)}, u32[]{:S(2)}, u32[]{:S(2)}) collective-permute-start(bf16[2,8,128,128]{3,2,1,0:T(8,128)(2,1)S(1)} %constant_dynamic-update-slice_fusion), channel_id=1, source_target_pairs={{0,8},{4,36},{8,16},{12,44},{16,24},{20,52},{24,0},{28,60},{32,40}... | collective-permute-start | bytes 1572872 | tf_op jit(solution)/shard_map/ppermute | solution.py:336
  20.9 4.9 %copy-start.2 = (s32[1,4]{0,1:T(4,128)S(1)}, s32[1,4]{0,1:T(4,128)}, u32[]{:S(2)}) copy-start(s32[1,4]{0,1:T(4,128)} %constant.169) | copy-start | bytes 52
  20.9 4.9 %copy-start.3 = (s32[1,4]{0,1:T(4,128)S(1)}, s32[1,4]{0,1:T(4,128)}, u32[]{:S(2)}) copy-start(s32[1,4]{0,1:T(4,128)} %constant.168) | copy-start | bytes 52
  20.9 5.5 %copy-start.4 = (s32[16,128]{1,0:T(8,128)S(1)}, s32[16,128]{1,0:T(8,128)}, u32[]{:S(2)}) copy-start(s32[16,128]{1,0:T(8,128)} %param.11) | copy-start | bytes 24580
  22.0 15.5 %collective-permute-start.5 = (bf16[32,128,128]{2,1,0:T(8,128)(2,1)}, bf16[32,128,128]{2,1,0:T(8,128)(2,1)}, u32[]{:S(2)}, u32[]{:S(2)}) collective-permute-start(bf16[32,128,128]{2,1,0:T(8,128)(2,1)} %pad_maximum_fusion.1.refs_0_), channel_id=1, source_target_pairs={{0,32},{4,12},{8,40},{12,20},{16,48},{20,28},{24,56},{28,4},{32,64... | collective-permute-start | bytes 3145736 | tf_op jit(solution)/shard_map/ppermute | solution.py:336
  24.3 14.3 %collective-permute-start.7 = (bf16[32,128,128]{2,1,0:T(8,128)(2,1)}, bf16[32,128,128]{2,1,0:T(8,128)(2,1)}, u32[]{:S(2)}, u32[]{:S(2)}) collective-permute-start(bf16[32,128,128]{2,1,0:T(8,128)(2,1)} %pad_maximum_fusion.2.refs_3_), channel_id=1, source_target_pairs={{0,96},{4,28},{8,104},{12,4},{16,112},{20,12},{24,120},{28,20},{32... | collective-permute-start | bytes 3145736 | tf_op jit(solution)/shard_map/ppermute | solution.py:336
  26.6 23.2 %collective-permute-start.9 = (bf16[32,128,128]{2,1,0:T(8,128)(2,1)}, bf16[32,128,128]{2,1,0:T(8,128)(2,1)}, u32[]{:S(2)}, u32[]{:S(2)}) collective-permute-start(bf16[32,128,128]{2,1,0:T(8,128)(2,1)} %pad_maximum_fusion.1.refs_0_), channel_id=1, source_target_pairs={{0,96},{4,28},{8,104},{12,4},{16,112},{20,12},{24,120},{28,20},{32... | collective-permute-start | bytes 3145736 | tf_op jit(solution)/shard_map/ppermute | solution.py:336
  28.0 21.8 %collective-permute-start.10 = (bf16[32,128,128]{2,1,0:T(8,128)(2,1)}, bf16[32,128,128]{2,1,0:T(8,128)(2,1)}, u32[]{:S(2)}, u32[]{:S(2)}) collective-permute-start(bf16[32,128,128]{2,1,0:T(8,128)(2,1)} %pad_maximum_fusion.2.refs_3_), channel_id=1, source_target_pairs={{0,32},{4,12},{8,40},{12,20},{16,48},{20,28},{24,56},{28,4},{32,64... | collective-permute-start | bytes 3145736 | tf_op jit(solution)/shard_map/ppermute | solution.py:336
  30.1 22.5 %collective-permute-start.2 = (bf16[8,512,128]{2,1,0:T(8,128)(2,1)S(1)}, bf16[8,512,128]{2,1,0:T(8,128)(2,1)}, u32[]{:S(2)}, u32[]{:S(2)}) collective-permute-start(bf16[8,512,128]{2,1,0:T(8,128)(2,1)S(1)} %get-tuple-element.16), channel_id=1, source_target_pairs={{0,4},{4,0},{8,12},{12,8},{16,20},{20,16},{24,28},{28,24},{32,36},... | collective-permute-start | bytes 3145736 | tf_op jit(solution)/shard_map/ppermute | solution.py:340
  37.5 22.5 %collective-permute-start.6 = (bf16[32,128,128]{2,1,0:T(8,128)(2,1)}, bf16[32,128,128]{2,1,0:T(8,128)(2,1)}, u32[]{:S(2)}, u32[]{:S(2)}) collective-permute-start(bf16[32,128,128]{2,1,0:T(8,128)(2,1)} %collective-permute-done.5.refs_1_), channel_id=1, source_target_pairs={{0,32},{4,12},{8,40},{12,20},{16,48},{20,28},{24,56},{28,4},{32,64... | collective-permute-start | bytes 3145736 | tf_op jit(solution)/shard_map/ppermute | solution.py:336
  38.6 22.5 %collective-permute-start.8 = (bf16[32,128,128]{2,1,0:T(8,128)(2,1)}, bf16[32,128,128]{2,1,0:T(8,128)(2,1)}, u32[]{:S(2)}, u32[]{:S(2)}) collective-permute-start(bf16[32,128,128]{2,1,0:T(8,128)(2,1)} %collective-permute-done.7.refs_5_), channel_id=1, source_target_pairs={{0,96},{4,28},{8,104},{12,4},{16,112},{20,12},{24,120},{28,20},{32... | collective-permute-start | bytes 3145736 | tf_op jit(solution)/shard_map/ppermute | solution.py:336
  66.8 6.6 %collective-permute-start.11 = (bf16[128,1024]{1,0:T(8,128)(2,1)S(1)}, bf16[128,1024]{1,0:T(8,128)(2,1)S(1)}, u32[]{:S(2)}, u32[]{:S(2)}) collective-permute-start(bf16[128,1024]{1,0:T(8,128)(2,1)S(1)} %get-tuple-element.20.after_ref.also_ref), channel_id=1, source_target_pairs={{0,4},{4,0},{8,12},{12,8},{16,20},{20,16},{24,28},{28,24},{32,36},... | collective-permute-start | bytes 786440 | tf_op jit(solution)/shard_map/ppermute | solution.py:340
  76.5 25.7 %collective-permute-start.14 = (bf16[128,4096]{1,0:T(8,128)(2,1)S(1)}, bf16[128,4096]{1,0:T(8,128)(2,1)S(1)}, u32[]{:S(2)}, u32[]{:S(2)}) collective-permute-start(bf16[128,4096]{1,0:T(8,128)(2,1)S(1)} %project_far.1.after_ref.also_ref), channel_id=1, source_target_pairs={{0,1},{1,2},{2,3},{3,0},{4,7},{5,4},{6,5},{7,6},{8,9},{9,10},{10,1... | collective-permute-start | bytes 3145736 | tf_op jit(solution)/shard_map/ppermute | solution.py:348
  83.8 4.7 %collective-permute-start.12 = (bf16[128,1024]{1,0:T(8,128)(2,1)S(1)}, bf16[128,1024]{1,0:T(8,128)(2,1)S(1)}, u32[]{:S(2)}, u32[]{:S(2)}) collective-permute-start(bf16[128,1024]{1,0:T(8,128)(2,1)S(1)} %near_theirs.1.after_ref.also_ref), channel_id=1, source_target_pairs={{0,4},{4,0},{8,12},{12,8},{16,20},{20,16},{24,28},{28,24},{32,36},... | collective-permute-start | bytes 786440 | tf_op jit(solution)/shard_map/ppermute | solution.py:340
  91.4 15.2 %collective-permute-start.15 = (bf16[128,4096]{1,0:T(8,128)(2,1)S(1)}, bf16[128,4096]{1,0:T(8,128)(2,1)S(1)}, u32[]{:S(2)}, u32[]{:S(2)}) collective-permute-start(bf16[128,4096]{1,0:T(8,128)(2,1)S(1)} %project_near.1.after_ref.also_ref), channel_id=1, source_target_pairs={{0,3},{1,0},{2,1},{3,2},{4,5},{5,6},{6,7},{7,4},{8,11},{9,8},{10,9... | collective-permute-start | bytes 3145736 | tf_op jit(solution)/shard_map/ppermute | solution.py:348
  96.2 6.0 %collective-permute-start.13 = (bf16[128,1024]{1,0:T(8,128)(2,1)S(1)}, bf16[128,1024]{1,0:T(8,128)(2,1)S(1)}, u32[]{:S(2)}, u32[]{:S(2)}) collective-permute-start(bf16[128,1024]{1,0:T(8,128)(2,1)S(1)} %last_theirs.1.after_ref.also_ref), channel_id=1, source_target_pairs={{0,4},{4,0},{8,12},{12,8},{16,20},{20,16},{24,28},{28,24},{32,36},... | collective-permute-start | bytes 786440 | tf_op jit(solution)/shard_map/ppermute | solution.py:340
  105.2 14.0 %collective-permute-start.17 = (bf16[128,4096]{1,0:T(8,128)(2,1)S(1)}, bf16[128,4096]{1,0:T(8,128)(2,1)S(1)}, u32[]{:S(2)}, u32[]{:S(2)}) collective-permute-start(bf16[128,4096]{1,0:T(8,128)(2,1)S(1)} %project_last.1.after_ref), channel_id=1, source_target_pairs={{0,1},{1,2},{2,3},{3,0},{4,7},{5,4},{6,5},{7,6},{8,9},{9,10},{10,1... | collective-permute-start | bytes 3145736 | tf_op jit(solution)/shard_map/ppermute | solution.py:348
  111.2 4.8 %collective-permute-start.16 = (bf16[128,1024]{1,0:T(8,128)(2,1)S(1)}, bf16[128,1024]{1,0:T(8,128)(2,1)S(1)}, u32[]{:S(2)}, u32[]{:S(2)}) collective-permute-start(bf16[128,1024]{1,0:T(8,128)(2,1)S(1)} %own_theirs.1.after_ref.also_ref), channel_id=1, source_target_pairs={{0,4},{4,0},{8,12},{12,8},{16,20},{20,16},{24,28},{28,24},{32,36},... | collective-permute-start | bytes 786440 | tf_op jit(solution)/shard_map/ppermute | solution.py:340
  116.0 4.4 %copy-start.1 = (s32[16,128,16]{1,2,0:T(8,128)S(1)}, s32[16,128,16]{1,2,0:T(8,128)}, u32[]{:S(2)}) copy-start(s32[16,128,16]{1,2,0:T(8,128)} %param.10) | copy-start | bytes 393220

commit v2 on v1

--- a/solution.py
+++ b/solution.py
@@ -16,6 +16,7 @@
 CORES = 2
 SEQ_DEVICES = RING * RING * CORES
 SIDE_COUPLES = 4
+PEELED = ("near_theirs", "near_mine", "last_theirs", "last_mine")
 CHUNK_COUPLES = 2 * SIDE_COUPLES
 EXP2_SCALE = float(BLK ** -0.5 * math.log2(math.e))
 LOW = -1e30
@@ -96,7 +97,7 @@
         out_ref[:, cols] = attended
 
 
-def pipelined(first, score, weigh, buffers, rest):
+def pipelined(first, peel, score, weigh, buffers, rest):
     score_a, top_a, score_b, top_b = buffers
     score(first, score_a, top_a)
     for copy in rest:
@@ -112,7 +113,13 @@
         weigh(couple + 1, score_b, top_b)
         return carry
 
-    lax.fori_loop(0, SIDE_COUPLES // 2, step, 0)
+    if peel:
+        step(0, 0)
+        score(last, score_b, top_b)
+        weigh(last - 1, score_a, top_a)
+        weigh(last, score_b, top_b)
+    else:
+        lax.fori_loop(0, SIDE_COUPLES // 2, step, 0)
 
 
 BUFFERS = [pltpu.VMEM((SPAN, PAIR), jnp.float32), pltpu.VMEM((1, PAIR), jnp.float32)] * 2
@@ -201,7 +208,7 @@
     )(*map(stay, pieces))
 
 
-def attend_kernel(first, places, lists, counts, place, q_ref, after_ref, also_ref, *refs):
+def attend_kernel(name, first, places, lists, counts, place, q_ref, after_ref, also_ref, *refs):
     if places:
         pieces, refs = refs[: len(places)], refs[len(places) + 2 :]
         out_ref, keys, values, *buffers, sems = refs
@@ -219,7 +226,7 @@
         tiles, total = weigh_couple(couple, counts, score_ref, top_ref)
         combine_couple(couple, cat(tiles, 0), total, lists, values, out_ref)
 
-    pipelined(first, score, weigh, buffers, rest)
+    pipelined(first, name in PEELED, score, weigh, buffers, rest)
 
 
 def attend_call(
@@ -233,7 +240,7 @@
         scratch += [pltpu.SemaphoreType.DMA((len(pieces),))]
         aliases = {6 + len(pieces): 1, 7 + len(pieces): 2}
     return pl.pallas_call(
-        functools.partial(attend_kernel, chunk * CHUNK_COUPLES + side * SIDE_COUPLES, places),
+        functools.partial(attend_kernel, name, chunk * CHUNK_COUPLES + side * SIDE_COUPLES, places),
         name=name,
         grid_spec=pltpu.PrefetchScalarGridSpec(
             num_scalar_prefetch=3,
@@ -285,17 +292,21 @@
 def project_kernel(kind, place, mine_ref, theirs_ref, held_ref, after_ref, *refs):
     out_ref = refs[-1]
     width = held_ref.shape[1]
-    tile = 1024
+    tile = 2048
     core = place[0]
     mine = mine_ref[...]
     theirs = theirs_ref[...]
     both = cat([jnp.where(core == 0, mine, theirs), jnp.where(core == 0, theirs, mine)], 1)
-    for at in range(0, width, tile):
-        cols = slice(at, at + tile)
+
+    def step(index, carry):
+        cols = pl.ds(pl.multiple_of(index * tile, tile), tile)
         total = jnp.dot(both, held_ref[:, cols], preferred_element_type=jnp.float32)
         if kind in ("last", "own"):
             total = total + refs[0][:, cols].astype(jnp.float32)
         out_ref[:, cols] = total.astype(out_ref.dtype)
+        return carry
+
+    lax.fori_loop(0, width // tile, step, 0)
 
 
 def project_call(kind, place, mine, theirs, held, after, *arrived):

time: 121 us -> 120 us (level)
  Pallas kernels: 61.4 us -> 60 us
    pallas_call x8, Pallas kernels: 37.6 us -> 35.3 us  [attend_call(): pl.pallas_call(functools.partial(attend_kernel, name, chunk * CHUNK_COUPL...]
  transfers between devices with their start and end apart: 18 -> 18, of which waited for: 9 -> 9; matrix products, arithmetic and copies ran while one was open for 4% -> 4% of each run, Pallas kernels for 43% -> 42%
where the time goes in v2:
time: 120 us
  Pallas kernels  60 us (50%)
  waiting for transfers between devices  27.1 us (23%)
  starting transfers between devices  24.5 us (20%)
  other arithmetic  5.44 us (5%)
  local copies, waits for them, and re-layouts  2.19 us (2%)
    pallas_call x8, Pallas kernels, attend_call(): pl.pallas_call(functools.partial(attend_kernel, name, chunk * CHUNK_COUPL...  35.3 us
    ppermute x9, waiting for transfers between devices, along(): return lax.ppermute(array, 'seq', chip_perm(phase, step))  25.4 us
    pallas_call x4, Pallas kernels, project_call(): pl.pallas_call(functools.partial(project_kernel, kind), name='project_' +...  12.8 us
    ppermute x9, starting transfers between devices, along(): return lax.ppermute(array, 'seq', chip_perm(phase, step))  12.1 us
    ppermute x6, starting transfers between devices, swap(): return lax.ppermute(array, 'seq', SWAP)  7.96 us
    pallas_call x1, Pallas kernels, hold_call(): pl.pallas_call(hold_kernel, name='hold_weight', in_specs=[HBM, HBM], out_...  5.78 us
    ppermute x3, starting transfers between devices, turn(): return lax.ppermute(array, ('seq', 'grp'), pairs)  4.46 us
    pallas_call x1, Pallas kernels, tables_call(): pl.pallas_call(functools.partial(tables_kernel, places), name='tables', i...  2.85 us
  transfers between devices with their start and end apart: 18, of which 9 were waited for; matrix products, arithmetic and copies ran while one was open for 4% of the time, Pallas kernels for 42%

profile of v2, /device:TPU:1, one launch (start us, length us, event | category | flops | bytes accessed | tf_op | source)
XLA Modules:
  0.0 119.7 jit_solution(8107171189925230506)
XLA Ops:
  0.0 1.2 %prepare.1 = (bf16[2,4,128,128]{3,2,1,0:T(8,128)(2,1)S(1)}, bf16[2,4,128,128]{3,2,1,0:T(8,128)(2,1)S(1)}) custom-call(bf16[2,512,128]{2,1,0:T(8,128)(2,1)} %key_ref.1, bf16[2,512,128]{2,1,0:T(8,128)(2,1)} %value_ref.1), custom_call_target="tpu_custom_call" | custom-call | flops 1 | bytes 1 | tf_op jit(solution)/shard_map/prepare/pallas_call | solution.py:166
  1.2 1.5 %collective-permute-start = (bf16[2,4,128,128]{3,2,1,0:T(8,128)(2,1)S(1)}, bf16[2,4,128,128]{3,2,1,0:T(8,128)(2,1)S(1)}, u32[]{:S(2)}, u32[]{:S(2)}) collective-permute-start(bf16[2,4,128,128]{3,2,1,0:T(8,128)(2,1)S(1)} %get-tuple-element.15), channel_id=1, source_target_pairs={{0,4},{4,0},{8,12},{12,8},{16,20},{20,16},{24,28},{28,24},{32,36},... | collective-permute-start | bytes 786440 | tf_op jit(solution)/shard_map/ppermute | solution.py:351
  3.9 3.8 %collective-permute-start.4 = (bf16[2,8,128,128]{3,2,1,0:T(8,128)(2,1)S(1)}, bf16[2,8,128,128]{3,2,1,0:T(8,128)(2,1)S(1)}, u32[]{:S(2)}, u32[]{:S(2)}) collective-permute-start(bf16[2,8,128,128]{3,2,1,0:T(8,128)(2,1)S(1)} %constant_dynamic-update-slice_fusion), channel_id=1, source_target_pairs={{0,16},{4,68},{8,24},{12,76},{16,0},{20,84},{24,8},{28,92},{32,48}... | collective-permute-start | bytes 1572872 | tf_op jit(solution)/shard_map/ppermute | solution.py:347
  9.2 5.4 %collective-permute-done.4 = bf16[2,8,128,128]{3,2,1,0:T(8,128)(2,1)S(1)} collective-permute-done((bf16[2,8,128,128]{3,2,1,0:T(8,128)(2,1)S(1)}, bf16[2,8,128,128]{3,2,1,0:T(8,128)(2,1)S(1)}, u32[]{:S(2)}, u32[]{:S(2)}) %collective-permute-start.4) | collective-permute-done | bytes 524320 | tf_op jit(solution)/shard_map/ppermute | solution.py:347
  14.6 6.1 %collective-permute-done.3 = bf16[2,8,128,128]{3,2,1,0:T(8,128)(2,1)S(1)} collective-permute-done((bf16[2,8,128,128]{3,2,1,0:T(8,128)(2,1)S(1)}, bf16[2,8,128,128]{3,2,1,0:T(8,128)(2,1)S(1)}, u32[]{:S(2)}, u32[]{:S(2)}) %collective-permute-start.3) | collective-permute-done | bytes 524320 | tf_op jit(solution)/shard_map/ppermute | solution.py:347
  24.3 1.5 %collective-permute-start.7 = (bf16[32,128,128]{2,1,0:T(8,128)(2,1)}, bf16[32,128,128]{2,1,0:T(8,128)(2,1)}, u32[]{:S(2)}, u32[]{:S(2)}) collective-permute-start(bf16[32,128,128]{2,1,0:T(8,128)(2,1)} %pad_maximum_fusion.2.refs_3_), channel_id=1, source_target_pairs={{0,96},{4,28},{8,104},{12,4},{16,112},{20,12},{24,120},{28,20},{32... | collective-permute-start | bytes 3145736 | tf_op jit(solution)/shard_map/ppermute | solution.py:347
  26.6 1.4 %collective-permute-start.9 = (bf16[32,128,128]{2,1,0:T(8,128)(2,1)}, bf16[32,128,128]{2,1,0:T(8,128)(2,1)}, u32[]{:S(2)}, u32[]{:S(2)}) collective-permute-start(bf16[32,128,128]{2,1,0:T(8,128)(2,1)} %pad_maximum_fusion.1.refs_0_), channel_id=1, source_target_pairs={{0,96},{4,28},{8,104},{12,4},{16,112},{20,12},{24,120},{28,20},{32... | collective-permute-start | bytes 3145736 | tf_op jit(solution)/shard_map/ppermute | solution.py:347
  28.0 2.1 %queries.1 = (bf16[8,512,128]{2,1,0:T(8,128)(2,1)S(1)}, bf16[8,512,128]{2,1,0:T(8,128)(2,1)S(1)}) custom-call(s32[9]{0:T(128)S(1)} %pad_add_fusion.place, bf16[16,512,128]{2,1,0:T(8,128)(2,1)} %source_ref.2, bf16[2,8,128,128]{3,2,1,0:T(8,128)(2,1)S(1)} %collective-permute-done.1.after_ref), custom_call_target="tpu_custom_call" | custom-call | flops 1 | bytes 1 | tf_op jit(solution)/shard_map/queries/pallas_call | solution.py:276
  30.1 2.4 %collective-permute-start.2 = (bf16[8,512,128]{2,1,0:T(8,128)(2,1)S(1)}, bf16[8,512,128]{2,1,0:T(8,128)(2,1)}, u32[]{:S(2)}, u32[]{:S(2)}) collective-permute-start(bf16[8,512,128]{2,1,0:T(8,128)(2,1)S(1)} %get-tuple-element.16), channel_id=1, source_target_pairs={{0,4},{4,0},{8,12},{12,8},{16,20},{20,16},{24,28},{28,24},{32,36},... | collective-permute-start | bytes 3145736 | tf_op jit(solution)/shard_map/ppermute | solution.py:351
  32.5 4.9 %collective-permute-done.5.refs_1_ = bf16[32,128,128]{2,1,0:T(8,128)(2,1)} collective-permute-done((bf16[32,128,128]{2,1,0:T(8,128)(2,1)}, bf16[32,128,128]{2,1,0:T(8,128)(2,1)}, u32[]{:S(2)}, u32[]{:S(2)}) %collective-permute-start.5) | collective-permute-done | bytes 1048608 | tf_op jit(solution)/shard_map/ppermute | solution.py:347
  38.6 2.7 %collective-permute-start.8 = (bf16[32,128,128]{2,1,0:T(8,128)(2,1)}, bf16[32,128,128]{2,1,0:T(8,128)(2,1)}, u32[]{:S(2)}, u32[]{:S(2)}) collective-permute-start(bf16[32,128,128]{2,1,0:T(8,128)(2,1)} %collective-permute-done.7.refs_5_), channel_id=1, source_target_pairs={{0,96},{4,28},{8,104},{12,4},{16,112},{20,12},{24,120},{28,20},{32... | collective-permute-start | bytes 3145736 | tf_op jit(solution)/shard_map/ppermute | solution.py:347
  43.1 5.8 %hold_weight.1.after_ref.also_ref.held_ref = bf16[2048,4096]{1,0:T(8,128)(2,1)S(1)} custom-call(bf16[2048,4096]{1,0:T(8,128)(2,1)} %source_ref.3, bf16[2,8,128,128]{3,2,1,0:T(8,128)(2,1)S(1)} %collective-permute-done.1.after_ref), custom_call_target="tpu_custom_call" | custom-call | tf_op jit(solution)/shard_map/hold_weight/pallas_call | solution.py:135
  49.8 2.9 %tables.1 = (bf16[128,128,128]{2,1,0:T(8,128)(2,1)S(1)}, bf16[128,128,128]{2,1,0:T(8,128)(2,1)S(1)}) custom-call(bf16[32,128,128]{2,1,0:T(8,128)(2,1)} %pad_maximum_fusion.1.refs_0_, bf16[32,128,128]{2,1,0:T(8,128)(2,1)} %collective-permute-done.5.refs_1_, bf16[32,128,128]{2,1,0:T(8,128)(2,1)} %collective-permute-done.9.refs_2_, ...), custom_call_target="tpu_custom_call" | custom-call | flops 1 | bytes 1 | tf_op jit(solution)/shard_map/tables/pallas_call | solution.py:199
  52.7 1.4 %pad_maximum_fusion.q_ref = bf16[2,8,512,128]{3,2,1,0:T(8,128)(2,1)S(1)} fusion(bf16[1,8,512,128]{3,2,1,0:T(8,128)(2,1)S(1)} %bitcast.24, bf16[1,8,512,128]{3,2,1,0:T(8,128)(2,1)} %bitcast.4), kind=kLoop, calls=%fused_computation.2 | loop fusion | flops 1048576 | bytes 4194304 | tf_op jit(solution)/shard_map/stack | solution.py:397
  54.1 5.8 %collective-permute-done.6.refs_0_ = bf16[32,128,128]{2,1,0:T(8,128)(2,1)} collective-permute-done((bf16[32,128,128]{2,1,0:T(8,128)(2,1)}, bf16[32,128,128]{2,1,0:T(8,128)(2,1)}, u32[]{:S(2)}, u32[]{:S(2)}) %collective-permute-start.6) | collective-permute-done | bytes 1048608 | tf_op jit(solution)/shard_map/ppermute | solution.py:347
  61.0 5.8 %far_theirs.1 = (bf16[128,1024]{1,0:T(8,128)(2,1)S(1)}, bf16[128,128,128]{2,1,0:T(8,128)(2,1)S(1)}, bf16[128,128,128]{2,1,0:T(8,128)(2,1)S(1)}) custom-call(s32[1024]{0:T(1024)S(1)} %reshape.71.lists, s32[64]{0:T(128)S(1)} %reshape.72.counts, s32[9]{0:T(128)S(1)} %pad_add_fusion.place, ...), custom_call_target="tpu_custom_call", output_to_operand_aliasing={{1}: (8, {}), {2}: (9, {})} | custom-call | flops 1 | bytes 1 | tf_op jit(solution)/shard_map/far_theirs/pallas_call | solution.py:242
  66.8 2.1 %collective-permute-start.11 = (bf16[128,1024]{1,0:T(8,128)(2,1)S(1)}, bf16[128,1024]{1,0:T(8,128)(2,1)S(1)}, u32[]{:S(2)}, u32[]{:S(2)}) collective-permute-start(bf16[128,1024]{1,0:T(8,128)(2,1)S(1)} %get-tuple-element.20.after_ref.also_ref), channel_id=1, source_target_pairs={{0,4},{4,0},{8,12},{12,8},{16,20},{20,16},{24,28},{28,24},{32,36},... | collective-permute-start | bytes 786440 | tf_op jit(solution)/shard_map/ppermute | solution.py:351
  68.9 4.5 %far_mine.1.mine_ref.after_ref = bf16[128,1024]{1,0:T(8,128)(2,1)S(1)} custom-call(s32[1024]{0:T(1024)S(1)} %reshape.71.lists, s32[64]{0:T(128)S(1)} %reshape.72.counts, s32[9]{0:T(128)S(1)} %pad_add_fusion.place, bf16[2,8,512,128]{3,2,1,0:T(8,128)(2,1)S(1)} %pad_maximum_fusion.q_ref, bf16[128,1024]{1,0:T(8,128)(2,1)S(1)} %get-tuple-element.20.after_ref.also_ref, ...), custom_call_target="tpu_custom_call" | custom-call | flops 1 | bytes 1 | tf_op jit(solution)/shard_map/far_mine/pallas_call | solution.py:242
  73.5 3.2 %project_far.1.after_ref.also_ref = bf16[128,4096]{1,0:T(8,128)(2,1)S(1)} custom-call(s32[9]{0:T(128)S(1)} %pad_add_fusion.place, bf16[128,1024]{1,0:T(8,128)(2,1)S(1)} %far_mine.1.mine_ref.after_ref, bf16[128,1024]{1,0:T(8,128)(2,1)S(1)} %collective-permute-done.11.theirs_ref, bf16[2048,4096]{1,0:T(8,128)(2,1)S(1)} %hold_weight.1.after_ref.also_ref.held_ref, ...), custom_call_target="tpu_custom_call" | custom-call | flops 1 | bytes 1 | tf_op jit(solution)/shard_map/project_far/pallas_call | solution.py:315
  76.7 2.7 %collective-permute-start.14 = (bf16[128,4096]{1,0:T(8,128)(2,1)S(1)}, bf16[128,4096]{1,0:T(8,128)(2,1)S(1)}, u32[]{:S(2)}, u32[]{:S(2)}) collective-permute-start(bf16[128,4096]{1,0:T(8,128)(2,1)S(1)} %project_far.1.after_ref.also_ref), channel_id=1, source_target_pairs={{0,1},{1,2},{2,3},{3,0},{4,7},{5,4},{6,5},{7,6},{8,9},{9,10},{10,1... | collective-permute-start | bytes 3145736 | tf_op jit(solution)/shard_map/ppermute | solution.py:359
  79.4 4.0 %near_theirs.1.after_ref.also_ref = bf16[128,1024]{1,0:T(8,128)(2,1)S(1)} custom-call(s32[1024]{0:T(1024)S(1)} %reshape.71.lists, s32[64]{0:T(128)S(1)} %reshape.72.counts, s32[9]{0:T(128)S(1)} %pad_add_fusion.place, bf16[2,8,512,128]{3,2,1,0:T(8,128)(2,1)S(1)} %pad_maximum_fusion.q_ref, bf16[128,4096]{1,0:T(8,128)(2,1)S(1)} %project_far.1.after_ref.also_ref, ...), custom_call_target="tpu_custom_call" | custom-call | flops 1 | bytes 1 | tf_op jit(solution)/shard_map/near_theirs/pallas_call | solution.py:242
  83.5 4.0 %near_mine.1.mine_ref.after_ref = bf16[128,1024]{1,0:T(8,128)(2,1)S(1)} custom-call(s32[1024]{0:T(1024)S(1)} %reshape.71.lists, s32[64]{0:T(128)S(1)} %reshape.72.counts, s32[9]{0:T(128)S(1)} %pad_add_fusion.place, bf16[2,8,512,128]{3,2,1,0:T(8,128)(2,1)S(1)} %pad_maximum_fusion.q_ref, bf16[128,1024]{1,0:T(8,128)(2,1)S(1)} %near_theirs.1.after_ref.also_ref, ...), custom_call_target="tpu_custom_call" | custom-call | flops 1 | bytes 1 | tf_op jit(solution)/shard_map/near_mine/pallas_call | solution.py:242
  87.4 3.2 %project_near.1.after_ref.also_ref = bf16[128,4096]{1,0:T(8,128)(2,1)S(1)} custom-call(s32[9]{0:T(128)S(1)} %pad_add_fusion.place, bf16[128,1024]{1,0:T(8,128)(2,1)S(1)} %near_mine.1.mine_ref.after_ref, bf16[128,1024]{1,0:T(8,128)(2,1)S(1)} %collective-permute-done.12.theirs_ref, bf16[2048,4096]{1,0:T(8,128)(2,1)S(1)} %hold_weight.1.after_ref.also_ref.held_ref, ...), custom_call_target="tpu_custom_call" | custom-call | flops 1 | bytes 1 | tf_op jit(solution)/shard_map/project_near/pallas_call | solution.py:315
  90.9 4.0 %last_theirs.1.after_ref.also_ref = bf16[128,1024]{1,0:T(8,128)(2,1)S(1)} custom-call(s32[1024]{0:T(1024)S(1)} %reshape.71.lists, s32[64]{0:T(128)S(1)} %reshape.72.counts, s32[9]{0:T(128)S(1)} %pad_add_fusion.place, bf16[2,8,512,128]{3,2,1,0:T(8,128)(2,1)S(1)} %pad_maximum_fusion.q_ref, bf16[128,4096]{1,0:T(8,128)(2,1)S(1)} %project_near.1.after_ref.also_ref, ...), custom_call_target="tpu_custom_call" | custom-call | flops 1 | bytes 1 | tf_op jit(solution)/shard_map/last_theirs/pallas_call | solution.py:242
  94.9 1.4 %collective-permute-start.13 = (bf16[128,1024]{1,0:T(8,128)(2,1)S(1)}, bf16[128,1024]{1,0:T(8,128)(2,1)S(1)}, u32[]{:S(2)}, u32[]{:S(2)}) collective-permute-start(bf16[128,1024]{1,0:T(8,128)(2,1)S(1)} %last_theirs.1.after_ref.also_ref), channel_id=1, source_target_pairs={{0,4},{4,0},{8,12},{12,8},{16,20},{20,16},{24,28},{28,24},{32,36},... | collective-permute-start | bytes 786440 | tf_op jit(solution)/shard_map/ppermute | solution.py:351
  96.3 4.0 %last_mine.1.mine_ref.after_ref = bf16[128,1024]{1,0:T(8,128)(2,1)S(1)} custom-call(s32[1024]{0:T(1024)S(1)} %reshape.71.lists, s32[64]{0:T(128)S(1)} %reshape.72.counts, s32[9]{0:T(128)S(1)} %pad_add_fusion.place, bf16[2,8,512,128]{3,2,1,0:T(8,128)(2,1)S(1)} %pad_maximum_fusion.q_ref, bf16[128,1024]{1,0:T(8,128)(2,1)S(1)} %last_theirs.1.after_ref.also_ref, ...), custom_call_target="tpu_custom_call" | custom-call | flops 1 | bytes 1 | tf_op jit(solution)/shard_map/last_mine/pallas_call | solution.py:242
  100.3 3.2 %project_last.1.after_ref = bf16[128,4096]{1,0:T(8,128)(2,1)S(1)} custom-call(s32[9]{0:T(128)S(1)} %pad_add_fusion.place, bf16[128,1024]{1,0:T(8,128)(2,1)S(1)} %last_mine.1.mine_ref.after_ref, bf16[128,1024]{1,0:T(8,128)(2,1)S(1)} %collective-permute-done.13.theirs_ref, bf16[2048,4096]{1,0:T(8,128)(2,1)S(1)} %hold_weight.1.after_ref.also_ref.held_ref, ...), custom_call_target="tpu_custom_call" | custom-call | flops 1 | bytes 1 | tf_op jit(solution)/shard_map/project_last/pallas_call | solution.py:315
  103.5 1.5 %collective-permute-start.17 = (bf16[128,4096]{1,0:T(8,128)(2,1)S(1)}, bf16[128,4096]{1,0:T(8,128)(2,1)S(1)}, u32[]{:S(2)}, u32[]{:S(2)}) collective-permute-start(bf16[128,4096]{1,0:T(8,128)(2,1)S(1)} %project_last.1.after_ref), channel_id=1, source_target_pairs={{0,1},{1,2},{2,3},{3,0},{4,7},{5,4},{6,5},{7,6},{8,9},{9,10},{10,1... | collective-permute-start | bytes 3145736 | tf_op jit(solution)/shard_map/ppermute | solution.py:359
  105.6 4.5 %own_theirs.1.after_ref.also_ref = bf16[128,1024]{1,0:T(8,128)(2,1)S(1)} custom-call(s32[1024]{0:T(1024)S(1)} %reshape.71.lists, s32[64]{0:T(128)S(1)} %reshape.72.counts, s32[9]{0:T(128)S(1)} %pad_add_fusion.place, bf16[2,8,512,128]{3,2,1,0:T(8,128)(2,1)S(1)} %pad_maximum_fusion.q_ref, bf16[128,4096]{1,0:T(8,128)(2,1)S(1)} %project_last.1.after_ref, ...), custom_call_target="tpu_custom_call" | custom-call | flops 1 | bytes 1 | tf_op jit(solution)/shard_map/own_theirs/pallas_call | solution.py:242
  110.6 4.5 %own_mine.1.mine_ref.after_ref = bf16[128,1024]{1,0:T(8,128)(2,1)S(1)} custom-call(s32[1024]{0:T(1024)S(1)} %reshape.71.lists, s32[64]{0:T(128)S(1)} %reshape.72.counts, s32[9]{0:T(128)S(1)} %pad_add_fusion.place, bf16[2,8,512,128]{3,2,1,0:T(8,128)(2,1)S(1)} %pad_maximum_fusion.q_ref, bf16[128,1024]{1,0:T(8,128)(2,1)S(1)} %own_theirs.1.after_ref.also_ref, ...), custom_call_target="tpu_custom_call" | custom-call | flops 1 | bytes 1 | tf_op jit(solution)/shard_map/own_mine/pallas_call | solution.py:242
  115.2 3.2 %project_own.1 = f32[128,4096]{1,0:T(8,128)S(1)} custom-call(s32[9]{0:T(128)S(1)} %pad_add_fusion.place, bf16[128,1024]{1,0:T(8,128)(2,1)S(1)} %own_mine.1.mine_ref.after_ref, bf16[128,1024]{1,0:T(8,128)(2,1)S(1)} %collective-permute-done.16.theirs_ref, bf16[2048,4096]{1,0:T(8,128)(2,1)S(1)} %hold_weight.1.after_ref.also_ref.held_ref, ...), custom_call_target="tpu_custom_call" | custom-call | flops 2000000000 | bytes 10000000 | tf_op jit(solution)/shard_map/project_own/pallas_call | solution.py:315
  118.4 1.2 %add_convert_fusion = bf16[128,4096]{1,0:T(8,128)(2,1)} fusion(f32[128,4096]{1,0:T(8,128)S(1)} %project_own.1, bf16[128,4096]{1,0:T(8,128)(2,1)S(1)} %collective-permute-done.17), kind=kLoop, calls=%fused_computation.3 | loop fusion | flops 1572864 | bytes 4194304 | tf_op jit(solution)/shard_map/convert_element_type | solution.py:451
  (62 shorter events, 13.4 us)
Async XLA Ops:
  0.0 42.0 %copy-start = (s32[16,128,16]{1,2,0:T(8,128)S(1)}, s32[16,128,16]{1,2,0:T(8,128)}, u32[]{:S(2)}) copy-start(s32[16,128,16]{1,2,0:T(8,128)} %param.10) | copy-start | bytes 393220
  1.2 2.7 %collective-permute-start = (bf16[2,4,128,128]{3,2,1,0:T(8,128)(2,1)S(1)}, bf16[2,4,128,128]{3,2,1,0:T(8,128)(2,1)S(1)}, u32[]{:S(2)}, u32[]{:S(2)}) collective-permute-start(bf16[2,4,128,128]{3,2,1,0:T(8,128)(2,1)S(1)} %get-tuple-element.15), channel_id=1, source_target_pairs={{0,4},{4,0},{8,12},{12,8},{16,20},{20,16},{24,28},{28,24},{32,36},... | collective-permute-start | bytes 786440 | tf_op jit(solution)/shard_map/ppermute | solution.py:351
  3.9 10.7 %collective-permute-start.4 = (bf16[2,8,128,128]{3,2,1,0:T(8,128)(2,1)S(1)}, bf16[2,8,128,128]{3,2,1,0:T(8,128)(2,1)S(1)}, u32[]{:S(2)}, u32[]{:S(2)}) collective-permute-start(bf16[2,8,128,128]{3,2,1,0:T(8,128)(2,1)S(1)} %constant_dynamic-update-slice_fusion), channel_id=1, source_target_pairs={{0,16},{4,68},{8,24},{12,76},{16,0},{20,84},{24,8},{28,92},{32,48}... | collective-permute-start | bytes 1572872 | tf_op jit(solution)/shard_map/ppermute | solution.py:347
  7.7 13.1 %collective-permute-start.3 = (bf16[2,8,128,128]{3,2,1,0:T(8,128)(2,1)S(1)}, bf16[2,8,128,128]{3,2,1,0:T(8,128)(2,1)S(1)}, u32[]{:S(2)}, u32[]{:S(2)}) collective-permute-start(bf16[2,8,128,128]{3,2,1,0:T(8,128)(2,1)S(1)} %constant_dynamic-update-slice_fusion), channel_id=1, source_target_pairs={{0,24},{4,100},{8,0},{12,108},{16,8},{20,116},{24,16},{28,124},{32... | collective-permute-start | bytes 1572872 | tf_op jit(solution)/shard_map/ppermute | solution.py:347
  8.1 12.7 %collective-permute-start.1 = (bf16[2,8,128,128]{3,2,1,0:T(8,128)(2,1)S(1)}, bf16[2,8,128,128]{3,2,1,0:T(8,128)(2,1)S(1)}, u32[]{:S(2)}, u32[]{:S(2)}) collective-permute-start(bf16[2,8,128,128]{3,2,1,0:T(8,128)(2,1)S(1)} %constant_dynamic-update-slice_fusion), channel_id=1, source_target_pairs={{0,8},{4,36},{8,16},{12,44},{16,24},{20,52},{24,0},{28,60},{32,40}... | collective-permute-start | bytes 1572872 | tf_op jit(solution)/shard_map/ppermute | solution.py:347
  20.9 4.9 %copy-start.2 = (s32[1,4]{0,1:T(4,128)S(1)}, s32[1,4]{0,1:T(4,128)}, u32[]{:S(2)}) copy-start(s32[1,4]{0,1:T(4,128)} %constant.169) | copy-start | bytes 52
  20.9 4.9 %copy-start.3 = (s32[1,4]{0,1:T(4,128)S(1)}, s32[1,4]{0,1:T(4,128)}, u32[]{:S(2)}) copy-start(s32[1,4]{0,1:T(4,128)} %constant.168) | copy-start | bytes 52
  20.9 5.5 %copy-start.4 = (s32[16,128]{1,0:T(8,128)S(1)}, s32[16,128]{1,0:T(8,128)}, u32[]{:S(2)}) copy-start(s32[16,128]{1,0:T(8,128)} %param.11) | copy-start | bytes 24580
  22.0 15.5 %collective-permute-start.5 = (bf16[32,128,128]{2,1,0:T(8,128)(2,1)}, bf16[32,128,128]{2,1,0:T(8,128)(2,1)}, u32[]{:S(2)}, u32[]{:S(2)}) collective-permute-start(bf16[32,128,128]{2,1,0:T(8,128)(2,1)} %pad_maximum_fusion.1.refs_0_), channel_id=1, source_target_pairs={{0,32},{4,12},{8,40},{12,20},{16,48},{20,28},{24,56},{28,4},{32,64... | collective-permute-start | bytes 3145736 | tf_op jit(solution)/shard_map/ppermute | solution.py:347
  24.3 14.3 %collective-permute-start.7 = (bf16[32,128,128]{2,1,0:T(8,128)(2,1)}, bf16[32,128,128]{2,1,0:T(8,128)(2,1)}, u32[]{:S(2)}, u32[]{:S(2)}) collective-permute-start(bf16[32,128,128]{2,1,0:T(8,128)(2,1)} %pad_maximum_fusion.2.refs_3_), channel_id=1, source_target_pairs={{0,96},{4,28},{8,104},{12,4},{16,112},{20,12},{24,120},{28,20},{32... | collective-permute-start | bytes 3145736 | tf_op jit(solution)/shard_map/ppermute | solution.py:347
  26.6 23.2 %collective-permute-start.9 = (bf16[32,128,128]{2,1,0:T(8,128)(2,1)}, bf16[32,128,128]{2,1,0:T(8,128)(2,1)}, u32[]{:S(2)}, u32[]{:S(2)}) collective-permute-start(bf16[32,128,128]{2,1,0:T(8,128)(2,1)} %pad_maximum_fusion.1.refs_0_), channel_id=1, source_target_pairs={{0,96},{4,28},{8,104},{12,4},{16,112},{20,12},{24,120},{28,20},{32... | collective-permute-start | bytes 3145736 | tf_op jit(solution)/shard_map/ppermute | solution.py:347
  28.0 21.8 %collective-permute-start.10 = (bf16[32,128,128]{2,1,0:T(8,128)(2,1)}, bf16[32,128,128]{2,1,0:T(8,128)(2,1)}, u32[]{:S(2)}, u32[]{:S(2)}) collective-permute-start(bf16[32,128,128]{2,1,0:T(8,128)(2,1)} %pad_maximum_fusion.2.refs_3_), channel_id=1, source_target_pairs={{0,32},{4,12},{8,40},{12,20},{16,48},{20,28},{24,56},{28,4},{32,64... | collective-permute-start | bytes 3145736 | tf_op jit(solution)/shard_map/ppermute | solution.py:347
  30.1 22.5 %collective-permute-start.2 = (bf16[8,512,128]{2,1,0:T(8,128)(2,1)S(1)}, bf16[8,512,128]{2,1,0:T(8,128)(2,1)}, u32[]{:S(2)}, u32[]{:S(2)}) collective-permute-start(bf16[8,512,128]{2,1,0:T(8,128)(2,1)S(1)} %get-tuple-element.16), channel_id=1, source_target_pairs={{0,4},{4,0},{8,12},{12,8},{16,20},{20,16},{24,28},{28,24},{32,36},... | collective-permute-start | bytes 3145736 | tf_op jit(solution)/shard_map/ppermute | solution.py:351
  37.5 22.5 %collective-permute-start.6 = (bf16[32,128,128]{2,1,0:T(8,128)(2,1)}, bf16[32,128,128]{2,1,0:T(8,128)(2,1)}, u32[]{:S(2)}, u32[]{:S(2)}) collective-permute-start(bf16[32,128,128]{2,1,0:T(8,128)(2,1)} %collective-permute-done.5.refs_1_), channel_id=1, source_target_pairs={{0,32},{4,12},{8,40},{12,20},{16,48},{20,28},{24,56},{28,4},{32,64... | collective-permute-start | bytes 3145736 | tf_op jit(solution)/shard_map/ppermute | solution.py:347
  38.6 22.5 %collective-permute-start.8 = (bf16[32,128,128]{2,1,0:T(8,128)(2,1)}, bf16[32,128,128]{2,1,0:T(8,128)(2,1)}, u32[]{:S(2)}, u32[]{:S(2)}) collective-permute-start(bf16[32,128,128]{2,1,0:T(8,128)(2,1)} %collective-permute-done.7.refs_5_), channel_id=1, source_target_pairs={{0,96},{4,28},{8,104},{12,4},{16,112},{20,12},{24,120},{28,20},{32... | collective-permute-start | bytes 3145736 | tf_op jit(solution)/shard_map/ppermute | solution.py:347
  66.8 6.6 %collective-permute-start.11 = (bf16[128,1024]{1,0:T(8,128)(2,1)S(1)}, bf16[128,1024]{1,0:T(8,128)(2,1)S(1)}, u32[]{:S(2)}, u32[]{:S(2)}) collective-permute-start(bf16[128,1024]{1,0:T(8,128)(2,1)S(1)} %get-tuple-element.20.after_ref.also_ref), channel_id=1, source_target_pairs={{0,4},{4,0},{8,12},{12,8},{16,20},{20,16},{24,28},{28,24},{32,36},... | collective-permute-start | bytes 786440 | tf_op jit(solution)/shard_map/ppermute | solution.py:351
  76.7 23.6 %collective-permute-start.14 = (bf16[128,4096]{1,0:T(8,128)(2,1)S(1)}, bf16[128,4096]{1,0:T(8,128)(2,1)S(1)}, u32[]{:S(2)}, u32[]{:S(2)}) collective-permute-start(bf16[128,4096]{1,0:T(8,128)(2,1)S(1)} %project_far.1.after_ref.also_ref), channel_id=1, source_target_pairs={{0,1},{1,2},{2,3},{3,0},{4,7},{5,4},{6,5},{7,6},{8,9},{9,10},{10,1... | collective-permute-start | bytes 3145736 | tf_op jit(solution)/shard_map/ppermute | solution.py:359
  83.4 4.1 %collective-permute-start.12 = (bf16[128,1024]{1,0:T(8,128)(2,1)S(1)}, bf16[128,1024]{1,0:T(8,128)(2,1)S(1)}, u32[]{:S(2)}, u32[]{:S(2)}) collective-permute-start(bf16[128,1024]{1,0:T(8,128)(2,1)S(1)} %near_theirs.1.after_ref.also_ref), channel_id=1, source_target_pairs={{0,4},{4,0},{8,12},{12,8},{16,20},{20,16},{24,28},{28,24},{32,36},... | collective-permute-start | bytes 786440 | tf_op jit(solution)/shard_map/ppermute | solution.py:351
  90.6 14.9 %collective-permute-start.15 = (bf16[128,4096]{1,0:T(8,128)(2,1)S(1)}, bf16[128,4096]{1,0:T(8,128)(2,1)S(1)}, u32[]{:S(2)}, u32[]{:S(2)}) collective-permute-start(bf16[128,4096]{1,0:T(8,128)(2,1)S(1)} %project_near.1.after_ref.also_ref), channel_id=1, source_target_pairs={{0,3},{1,0},{2,1},{3,2},{4,5},{5,6},{6,7},{7,4},{8,11},{9,8},{10,9... | collective-permute-start | bytes 3145736 | tf_op jit(solution)/shard_map/ppermute | solution.py:359
  94.9 5.4 %collective-permute-start.13 = (bf16[128,1024]{1,0:T(8,128)(2,1)S(1)}, bf16[128,1024]{1,0:T(8,128)(2,1)S(1)}, u32[]{:S(2)}, u32[]{:S(2)}) collective-permute-start(bf16[128,1024]{1,0:T(8,128)(2,1)S(1)} %last_theirs.1.after_ref.also_ref), channel_id=1, source_target_pairs={{0,4},{4,0},{8,12},{12,8},{16,20},{20,16},{24,28},{28,24},{32,36},... | collective-permute-start | bytes 786440 | tf_op jit(solution)/shard_map/ppermute | solution.py:351
  103.5 14.9 %collective-permute-start.17 = (bf16[128,4096]{1,0:T(8,128)(2,1)S(1)}, bf16[128,4096]{1,0:T(8,128)(2,1)S(1)}, u32[]{:S(2)}, u32[]{:S(2)}) collective-permute-start(bf16[128,4096]{1,0:T(8,128)(2,1)S(1)} %project_last.1.after_ref), channel_id=1, source_target_pairs={{0,1},{1,2},{2,3},{3,0},{4,7},{5,4},{6,5},{7,6},{8,9},{9,10},{10,1... | collective-permute-start | bytes 3145736 | tf_op jit(solution)/shard_map/ppermute | solution.py:359
  110.1 5.1 %collective-permute-start.16 = (bf16[128,1024]{1,0:T(8,128)(2,1)S(1)}, bf16[128,1024]{1,0:T(8,128)(2,1)S(1)}, u32[]{:S(2)}, u32[]{:S(2)}) collective-permute-start(bf16[128,1024]{1,0:T(8,128)(2,1)S(1)} %own_theirs.1.after_ref.also_ref), channel_id=1, source_target_pairs={{0,4},{4,0},{8,12},{12,8},{16,20},{20,16},{24,28},{28,24},{32,36},... | collective-permute-start | bytes 786440 | tf_op jit(solution)/shard_map/ppermute | solution.py:351
  115.2 4.5 %copy-start.1 = (s32[16,128,16]{1,2,0:T(8,128)S(1)}, s32[16,128,16]{1,2,0:T(8,128)}, u32[]{:S(2)}) copy-start(s32[16,128,16]{1,2,0:T(8,128)} %param.10) | copy-start | bytes 393220
